TPU v7x, 512 devices: a whole 4x4x16 slice. The times are simulated.
512 devices in a mesh: chan: 8 (over x, z_hi), bl: 64 (over y, z_lo, core).
Axes of the slice: x: 4, y: 4, z: 16 (z_hi: 2, z_lo: 8; z = z_hi * 8 + z_lo), core: 2. Of those that a mesh axis runs over, the one named last changes fastest.
Arguments:
- measured_correlations: float32 [8, 4, 64, 32768], P(None, None, 'chan', 'bl'), may hold values from -6 to 6
- model_visibility: float32 [8, 4, 64, 32768], P(None, None, 'chan', 'bl'), may hold values from -6 to 6
- sample_importances: float32 [4, 64, 32768], P(None, 'chan', 'bl'), may hold values from 0.2 to 2
- rejected_frequency_tally: int32 [8, 32768], P('chan', 'bl'), may hold values from 0 to 4
- antenna_one: int32 [32768], P('bl'), may hold values from 0 to 511, as said below
- antenna_two: int32 [32768], P('bl'), may hold values from 0 to 511, as said below
- station_gains: float32 [8, 4, 64, 512], P(None, None, 'chan', 'bl'), may hold values from -3 to 3
- tv_weight: float32 [64, 512], P('chan', 'bl'), may hold values from 0.3 to 3
Outputs:
- updated_gains: float32 [8, 4, 64, 512], P(None, None, 'chan', 'bl')
- weighted_residual: float32 [8, 4, 64, 32768], P(None, None, 'chan', 'bl')
Inputs may be any that keep to these rules, and one draw needn't show every extreme that they name: `antenna_one`: station index of each baseline's first station. `antenna_two`: station index of each baseline's second station, never equal to antenna_one on the same baseline.
All inputs are finite; a program needn't handle non-finite values.
Results may differ from a plain program's by a relative error of at most 0.000098.
Values sent between devices are 32-bit elements; how exact they have to be, the bound alone decides.
A program may use at most 128 MiB of HBM per device.

v0:
```python
import jax
import jax.numpy as jnp
from jax import lax
from jax.sharding import PartitionSpec as P

STATION_COUNT = 512


smooth_eps = 0.01
tv_scale = 2.0


def with_halo(cells, sides, width):
    for axis, dim in sides:
        count = lax.axis_size(axis)
        ends = count - 1
        head = lax.slice_in_dim(cells, 0, width, axis=dim)
        tail = lax.slice_in_dim(cells, cells.shape[dim] - width, cells.shape[dim], axis=dim)
        cells = jnp.concatenate(
            [
                lax.ppermute(tail, axis, [(i, (i + 1) % count) for i in range(ends)]),
                cells,
                lax.ppermute(head, axis, [((i + 1) % count, i) for i in range(ends)]),
            ],
            axis=dim,
        )
    return cells


def complex_product(left, right):
    real_parts = []
    imag_parts = []
    for left_idx in range(2):
        for right_idx in range(2):
            leading_entry = 2 * left_idx
            second = 2 * left_idx + 1
            real_parts.append(
                left[leading_entry] * right[right_idx]
                - left[leading_entry + 4] * right[right_idx + 4]
                + left[second] * right[right_idx + 2]
                - left[second + 4] * right[right_idx + 6]
            )
            imag_parts.append(
                left[leading_entry] * right[right_idx + 4]
                + left[leading_entry + 4] * right[right_idx]
                + left[second] * right[right_idx + 6]
                + left[second + 4] * right[right_idx + 2]
            )
    return jnp.stack(real_parts + imag_parts)


def adjoint(matrix):
    return jnp.stack(
        [matrix[0], matrix[2], matrix[1], matrix[3], -matrix[4], -matrix[6], -matrix[5], -matrix[7]]
    )


def predicted(gain_first, model_part, gain_second):
    return complex_product(complex_product(gain_first, model_part), adjoint(gain_second))


def local(
    measured_correlations,
    model_visibility,
    sample_importances,
    rejected_frequency_tally,
    antenna_one,
    antenna_two,
    station_gains,
    tv_weight,
):
    frequency_group_size = measured_correlations.shape[2]
    pair_group_size = measured_correlations.shape[3]
    times_count = measured_correlations.shape[1]
    frequency_index_within = jnp.arange(frequency_group_size, dtype=jnp.int32)[:, None]
    accepted_sample_indicator = (
        frequency_index_within < frequency_group_size - rejected_frequency_tally
    ).astype(jnp.float32)
    nonzero_importance = sample_importances * accepted_sample_indicator[None]
    full_gains = lax.all_gather(station_gains, "bl", axis=3, tiled=True)
    gain_first = jnp.take(full_gains, antenna_one, axis=3)
    gain_second = jnp.take(full_gains, antenna_two, axis=3)

    def data_loss(leading_entry, second):
        diff = measured_correlations - predicted(leading_entry, model_visibility, second)
        return 0.5 * jnp.sum(nonzero_importance[None] * diff * diff)

    weighted_residual = nonzero_importance[None] * (
        measured_correlations - predicted(gain_first, model_visibility, gain_second)
    )
    value, pullback = jax.vjp(data_loss, gain_first, gain_second)
    grad_first, grad_second = pullback(jnp.ones_like(value))
    blank_table = jnp.zeros((8, times_count, frequency_group_size, STATION_COUNT), jnp.float32)
    station_table = (
        blank_table.at[:, :, :, antenna_one]
        .add(grad_first)
        .at[:, :, :, antenna_two]
        .add(grad_second)
    )
    owned_grad = lax.psum_scatter(station_table, "bl", scatter_dimension=3, tiled=True)
    weight_layer = jnp.broadcast_to(tv_weight[None, None], (1, times_count) + tv_weight.shape)
    stacked = jnp.concatenate([station_gains, weight_layer], axis=0)
    padded = with_halo(stacked, (("chan", 2),), 1)
    padded_gain = padded[:8]
    padded_weight = padded[8, 0]
    block_index = lax.axis_index("chan")
    lower_ok = (block_index > 0).astype(jnp.float32)
    upper_ok = (block_index < lax.axis_size("chan") - 1).astype(jnp.float32)
    edge_index = jnp.arange(frequency_group_size + 1, dtype=jnp.int32)
    edge_mask = jnp.where(
        edge_index == 0, lower_ok, jnp.where(edge_index == frequency_group_size, upper_ok, 1.0)
    )
    edge_weight = padded_weight[1:] * edge_mask[:, None]

    def local_smooth(own_gain):
        extended = jnp.concatenate(
            [padded_gain[:, :, :1], own_gain, padded_gain[:, :, -1:]], axis=2
        )
        chan_step = extended[:, :, 1:] - extended[:, :, :-1]
        chan_term = jnp.sum(
            edge_weight * jnp.sqrt(jnp.sum(chan_step * chan_step, axis=0) + smooth_eps)
        )
        time_step = own_gain[:, 1:] - own_gain[:, :-1]
        time_term = jnp.sum(
            tv_weight * jnp.sqrt(jnp.sum(time_step * time_step, axis=0) + smooth_eps)
        )
        return chan_term + time_term

    smooth_grad = jax.grad(local_smooth)(station_gains)
    all_antenna_pairs = pair_group_size * lax.axis_size("bl")
    descent_scale = 2.0 * STATION_COUNT / all_antenna_pairs
    updated_gains = station_gains - descent_scale * (owned_grad + tv_scale * smooth_grad)
    return (updated_gains, weighted_residual)


def solution(mesh):
    placed = (
        P(None, None, "chan", "bl"),
        P(None, None, "chan", "bl"),
        P(None, "chan", "bl"),
        P("chan", "bl"),
        P("bl"),
        P("bl"),
        P(None, None, "chan", "bl"),
        P("chan", "bl"),
    )
    return jax.shard_map(
        local,
        mesh=mesh,
        in_specs=placed,
        out_specs=(P(None, None, "chan", "bl"), P(None, None, "chan", "bl")),
        check_vma=False,
    )
```

profile of v0, /device:TPU:1, one launch (start us, length us, event | category | flops | bytes accessed | tf_op | source)
XLA Modules:
  0.0 843.8 jit_solution(15931936747172999924)
XLA Ops:
  7.2 0.8 copy.203
  8.0 1.0 copy.204
  9.0 0.1 slice_maximum_fusion
  9.1 16.3 %collective-permute-start.1 = (f32[9,4,1,8]{2,3,1,0:T(8,128)S(1)}, f32[9,4,1,8]{2,3,1,0:T(8,128)S(1)}, u32[]{:S(2)}, u32[]{:S(2)}) collective-permute-start(f32[9,4,1,8]{2,3,1,0:T(8,128)S(1)} %get-tuple-element.153), channel_id=1, source_target_pairs={{0,64},{64,128},{128,192},{192,256},{256,320},{320,384},{384,448},... | collective-permute-start | bytes 3464 | tf_op jit(solution)/shard_map/ppermute | solution.py:21
  25.4 1.3 collective-permute-start
  26.7 1.0 copy.209
  27.7 0.7 compare_select_fusion
  28.4 0.7 compare_and_fusion
  29.1 0.7 compare_select_fusion.1
  29.7 0.7 compare_and_fusion.1
  30.4 180.0 %all_gather.3 = f32[8,4,8,512]{2,0,3,1:T(8,128)} all-gather(f32[8,4,8,8]{2,0,3,1:T(8,128)S(1)} %copy.209), channel_id=1, replica_groups=mesh['chan'=8,'bl'=64] {'bl'}, dimensions={3}, use_global_device_ids=true | all-gather | bytes 532480 | tf_op jit(solution)/shard_map/all_gather | solution.py:80
  210.4 8.3 gather_fusion.1
  218.7 5.2 copy.196
  223.9 8.3 gather_fusion
  232.2 5.2 copy.195
  237.4 0.1 select_bitcast_fusion
  237.5 0.1 subtract_dynamic-update-slice_fusion.3
  237.7 0.1 subtract_dynamic-update-slice_fusion.1
  238.1 1.0 add_negate_fusion
  239.1 0.1 slice_multiply_fusion.1
  239.1 0.1 slice_multiply_fusion.64
  239.3 0.1 slice_multiply_fusion.79
  239.3 0.2 pad_add_fusion.1
  239.6 0.1 slice_multiply_fusion.25
  239.7 0.1 negate_multiply_fusion.15
  239.8 0.1 slice_multiply_fusion.31
  239.9 0.1 slice_multiply_fusion.72
  240.0 0.1 slice_multiply_fusion.75
  240.1 0.2 add_bitcast_fusion.1
  240.4 7.4 copy.198
  247.7 0.2 pad_add_fusion
  248.0 0.3 add_bitcast_fusion
  248.3 7.4 copy.199
  255.7 3.8 broadcast_in_dim.32.clone
  259.5 67.4 %scatter_fusion = f32[8,4,8,512]{2,0,3,1:T(8,128)} fusion(f32[8,4,8,512]{2,0,3,1:T(8,128)} %broadcast_in_dim.32.clone, s32[512]{0:T(512)S(1)} %compare_select_fusion.1, f32[512,8,4,8]{3,1,2,0:T(8,128)} %copy.198), kind=kCustom, calls=%fused_computation.2 | custom fusion | flops 131072 | bytes 1574912 | tf_op jit(solution)/shard_map/scatter-add | solution.py:96
  326.9 67.4 %scatter_fusion.1 = f32[8,4,8,512]{2,0,3,1:T(8,128)} fusion(f32[8,4,8,512]{2,0,3,1:T(8,128)} %scatter_fusion, s32[512]{0:T(512)S(1)} %compare_select_fusion, f32[512,8,4,8]{3,1,2,0:T(8,128)} %copy.199), kind=kCustom, calls=%fused_computation.3 | custom fusion | flops 131072 | bytes 1574912 | tf_op jit(solution)/shard_map/scatter-add | solution.py:98
  394.3 7.8 copy.324
  402.1 7.7 reshape.103
  409.8 0.1 copy.202
  410.0 0.1 copy.207
  410.1 0.1 copy.206
  410.2 0.1 multiply_reduce_fusion
  410.3 0.1 fusion.8
  410.4 0.1 fusion.10
  410.6 424.7 %reduce-scatter.4.cloned.1.call-done = f32[8,256]{1,0:T(8,128)} async-done(((f32[512,256]{1,0:T(8,128)}), f32[8,256]{1,0:T(8,128)}) %reduce-scatter.4.cloned.1.call-update) | async-done | bytes 8208
  835.3 0.8 reshape.104
  836.1 0.1 fusion.4
  836.2 0.8 copy.210
  (40 shorter events, 0.7 us)
Async XLA Ops:
  7.2 828.1 %reduce-scatter.4.cloned.1.call-start = ((), (), s32[]{:S(2)}) async-start(), calls=%async_computation.1 | async-start | bytes 532480
  9.1 400.9 %collective-permute-start.1 = (f32[9,4,1,8]{2,3,1,0:T(8,128)S(1)}, f32[9,4,1,8]{2,3,1,0:T(8,128)S(1)}, u32[]{:S(2)}, u32[]{:S(2)}) collective-permute-start(f32[9,4,1,8]{2,3,1,0:T(8,128)S(1)} %get-tuple-element.153), channel_id=1, source_target_pairs={{0,64},{64,128},{128,192},{192,256},{256,320},{320,384},{384,448},... | collective-permute-start | bytes 3464 | tf_op jit(solution)/shard_map/ppermute | solution.py:21
  25.4 384.7 %collective-permute-start = (f32[9,4,1,8]{2,3,1,0:T(8,128)S(1)}, f32[9,4,1,8]{2,3,1,0:T(8,128)S(1)}, u32[]{:S(2)}, u32[]{:S(2)}) collective-permute-start(f32[9,4,1,8]{2,3,1,0:T(8,128)S(1)} %get-tuple-element.152), channel_id=1, source_target_pairs={{64,0},{128,64},{192,128},{256,192},{320,256},{384,320},{448,384},... | collective-permute-start | bytes 3464 | tf_op jit(solution)/shard_map/ppermute | solution.py:23
  30.4 193.5 %copy-start.4 = (s32[1,512]{1,0:T(1,128)S(1)}, s32[1,512]{1,0:T(1,128)}, u32[]{:S(2)}) copy-start(s32[1,512]{1,0:T(1,128)} %param.13) | copy-start | bytes 6148
  218.7 18.8 %copy-start = (f32[8,4,8,512]{3,2,1,0:T(8,128)S(1)}, f32[8,4,8,512]{3,2,1,0:T(8,128)}, u32[]{:S(2)}) copy-start(f32[8,4,8,512]{3,2,1,0:T(8,128)} %param.11) | copy-start | bytes 1572868
  232.2 5.8 copy-start.2
  232.2 5.9 copy-start.1
  240.0 8.0 copy-start.5
  402.1 7.7 copy-start.3
Sparse Core Ops, SparseCore 0:
  409.9 425.3 reduce-scatter.3
where the time goes:
time: 855 us; the launch traced here: 844 us
  waiting for transfers between devices  425 us (50%)
  blocking collectives  180 us (21%)
  other arithmetic  141 us (16%)
  local copies, waits for them, and re-layouts  65.5 us (8%)
  starting transfers between devices  17.6 us (2%)
  between operations  14.4 us (2%)
    unnamed x2, waiting for transfers between devices  425 us
    all_gather x1, blocking collectives, local(): full_gains = lax.all_gather(station_gains, 'bl', axis=3, tiled=True)  180 us
    scatter-add x2, other arithmetic, local(): station_table = blank_table.at[:, :, :, antenna_one].add(grad_first).at[:...  135 us
    unnamed x19, local copies, waits for them, and re-layouts  19.8 us
  transfers between devices with their start and end apart: 3, of which 1 were waited for; matrix products, arithmetic and copies ran while one was open for 24% of the time, Pallas kernels for 0%

commit v1 on v0

v1 whole, which is shorter than its diff:
```python
import jax
import jax.numpy as jnp
from jax import lax
from jax.experimental import pallas as pl
from jax.experimental.pallas import tpu as pltpu
from jax.sharding import PartitionSpec as P

MESH = pl.DeviceIdType.MESH
STATIONS = 512
BASELINES = 32768
TIMES = 4
CHANNELS = 8
PAIRS = 512
LANES = 8 * TIMES * CHANNELS
NY, NZ, NC = 4, 8, 2
SMOOTH_EPS = 0.01
TV_SCALE = 2.0
STEP = 2.0 * STATIONS / BASELINES
F32 = jnp.float32
BF16 = jnp.bfloat16


def cmul_add(terms):
    real, imag = None, None
    for (ar, ai), (br, bi), conj in terms:
        if conj:
            r, i = ar * br + ai * bi, ai * br - ar * bi
        else:
            r, i = ar * br - ai * bi, ar * bi + ai * br
        real = r if real is None else real + r
        imag = i if imag is None else imag + i
    return real, imag


def halves(x):
    high = x.astype(BF16)
    return high, (x - high.astype(F32)).astype(BF16)


def split_index():
    bl = lax.axis_index("bl")
    return lax.div(bl, NZ * NC), lax.rem(lax.div(bl, NC), NZ), lax.rem(bl, NC)


def join_index(y, z, core):
    return (y * NZ + z) * NC + core


def row_of(y, z, core):
    return pl.multiple_of(((core * NY + y) * NZ + z) * 8, 8)


def kernel(
    meas_h, model_h, imp_h, tally_h, one_h, two_h, gains_h, tvw_h,
    upd_ref, res_h,
    meas, model, imp, tally, one, two, gains, tvw,
    table, hot1, hot2, gp, gq, res, part, got_core, got_y, got_z, halo, halo_got, smooth, own_x,
    in_sem, out_sem, zs, zr, ys, yr, cs, cr, hs, hr, rcs, rcr, rys, ryr, rzs, rzr,
):
    chan = lax.axis_index("chan")
    y, z, core = split_index()
    n_chan = lax.axis_size("chan")

    def to_bl(src, dst, send, recv, peer):
        return pltpu.make_async_remote_copy(
            src_ref=src, dst_ref=dst, send_sem=send, recv_sem=recv,
            device_id={"bl": peer}, device_id_type=MESH,
        )

    z_peer = [None] + [join_index(y, lax.rem(z + k, NZ), core) for k in range(1, NZ)]
    y_peer = [None] + [join_index(lax.rem(y + k, NY), z, core) for k in range(1, NY)]
    other = join_index(y, z, 1 - core)
    chan_next = lax.rem(chan + 1, n_chan)
    chan_prev = lax.rem(chan + n_chan - 1, n_chan)

    loads = [
        pltpu.make_async_copy(src, dst, in_sem.at[i])
        for i, (src, dst) in enumerate(
            [(gains_h, gains), (one_h, one), (two_h, two), (tvw_h, tvw), (tally_h, tally),
             (imp_h, imp), (meas_h, meas), (model_h, model)]
        )
    ]
    loads[0].start()
    barrier = pltpu.get_barrier_semaphore()
    for peer in z_peer[1:] + y_peer[1:] + [other]:
        pl.semaphore_signal(barrier, inc=1, device_id={"bl": peer}, device_id_type=MESH)
    for peer in (chan_next, chan_prev):
        pl.semaphore_signal(barrier, inc=1, device_id={"chan": peer}, device_id_type=MESH)
    for load in loads[1:]:
        load.start()

    own_row = row_of(y, z, core)
    loads[0].wait()
    own = jnp.transpose(gains[...].reshape(LANES, 8))
    own_x[...] = own
    table[pl.ds(own_row, 8), :] = own
    pl.semaphore_wait(barrier, NZ + NY + 1)

    z_sends = []
    for k in range(1, NZ):
        rows = table.at[pl.ds(own_row, 8)]
        copy = to_bl(rows, rows, zs.at[k], zr.at[k], z_peer[k])
        copy.start()
        z_sends.append(copy)

    loads[1].wait()
    loads[2].wait()

    def to_row(ant):
        return (
            (lax.shift_right_logical(ant, 3) & 1) * 256
            + lax.shift_right_logical(ant, 7) * 64
            + (lax.shift_right_logical(ant, 4) & 7) * 8
            + (ant & 7)
        )

    row1, row2 = to_row(one[...]), to_row(two[...])

    def hot_body(i, carry):
        base = pl.multiple_of(i * 32, 32)
        index = lax.broadcasted_iota(jnp.int32, (32, PAIRS), 0) + base
        hot1[pl.ds(base, 32), :] = jnp.where(index == row1, 1.0, 0.0).astype(BF16)
        hot2[pl.ds(base, 32), :] = jnp.where(index == row2, 1.0, 0.0).astype(BF16)
        return carry

    lax.fori_loop(0, 8, hot_body, 0)

    for k in range(1, NZ):
        rows = table.at[pl.ds(row_of(y, lax.rem(z + NZ - k, NZ), core), 8)]
        to_bl(rows, rows, zs.at[k], zr.at[k], z_peer[k]).wait_recv()

    column = table.at[pl.ds(row_of(y, 0, core), 64)]
    y_sends = []
    for k in range(1, NY):
        copy = to_bl(column, column, ys.at[k], yr.at[k], y_peer[k])
        copy.start()
        y_sends.append(copy)
    c_sends = [to_bl(column, column, cs.at[0], cr.at[0], other)]
    c_sends[0].start()

    loads[3].wait()
    lane = lax.broadcasted_iota(jnp.int32, (8, LANES), 1)
    freq, time = lane & 7, lax.shift_right_logical(lane, 3) & 3
    weight = jnp.transpose(
        jnp.broadcast_to(tvw[...][None], (8 * TIMES, CHANNELS, 8)).reshape(LANES, 8)
    )
    low, high = own[:, :128], own[:, 128:]
    freq_h = freq[:, :128]
    halo[...] = jnp.where(
        freq_h == 0, low,
        jnp.where(
            freq_h == 1, pltpu.roll(high, 1, 1),
            jnp.where(
                freq_h == 7, low,
                jnp.where(freq_h == 6, pltpu.roll(high, 127, 1), pltpu.roll(weight[:, :128], 2, 1)),
            ),
        ),
    )
    h_sends = []
    for k, peer in enumerate((chan_next, chan_prev)):
        copy = pltpu.make_async_remote_copy(
            src_ref=halo, dst_ref=halo_got.at[k], send_sem=hs.at[k], recv_sem=hr.at[k],
            device_id={"chan": peer}, device_id_type=MESH,
        )
        copy.start()
        h_sends.append(copy)

    lax.fori_loop(8, 16, hot_body, 0)

    for k in range(1, NY):
        rows = table.at[pl.ds(row_of(lax.rem(y + NY - k, NY), 0, core), 64)]
        to_bl(rows, rows, ys.at[k], yr.at[k], y_peer[k]).wait_recv()
        copy = to_bl(rows, rows, cs.at[k], cr.at[k], other)
        copy.start()
        c_sends.append(copy)

    loads[4].wait()
    loads[5].wait()
    keep = lax.broadcasted_iota(jnp.int32, (CHANNELS, PAIRS), 0) < CHANNELS - tally[...]
    for t in range(TIMES):
        imp[t] = jnp.where(keep, imp[t], 0.0)

    for k in range(NY):
        rows = table.at[pl.ds(row_of(lax.rem(y + NY - k, NY), 0, 1 - core), 64)]
        to_bl(rows, rows, cs.at[k], cr.at[k], other).wait_recv()

    flipped = jnp.transpose(table[...])
    g_high, g_low = halves(flipped)
    for hot, dst in ((hot1, gp), (hot2, gq)):
        picked = jnp.dot(g_high, hot[...], preferred_element_type=F32) + jnp.dot(
            g_low, hot[...], preferred_element_type=F32
        )
        dst[...] = picked.reshape(8, TIMES, CHANNELS, PAIRS)
    loads[6].wait()
    loads[7].wait()

    def compute(i, carry):
        t = lax.div(i, 4)
        at = pl.ds(pl.multiple_of(lax.rem(i, 4) * 128, 128), 128)

        def matrix(ref):
            return [(ref[c, t, :, at], ref[c + 4, t, :, at]) for c in range(4)]

        jp, jq, m, d = matrix(gp), matrix(gq), matrix(model), matrix(meas)
        w = imp[t, :, at]
        a = [
            cmul_add([(jp[2 * r], m[c], False), (jp[2 * r + 1], m[c + 2], False)])
            for r in range(2) for c in range(2)
        ]
        v = [
            cmul_add([(a[2 * r], jq[2 * c], True), (a[2 * r + 1], jq[2 * c + 1], True)])
            for r in range(2) for c in range(2)
        ]
        e = [(w * (d[k][0] - v[k][0]), w * (d[k][1] - v[k][1])) for k in range(4)]
        for k in range(4):
            res[k, t, :, at] = e[k][0]
            res[k + 4, t, :, at] = e[k][1]
        b = [
            cmul_add([(jq[2 * r], m[2 * c], True), (jq[2 * r + 1], m[2 * c + 1], True)])
            for r in range(2) for c in range(2)
        ]
        first = [
            cmul_add([(e[2 * r], b[c], False), (e[2 * r + 1], b[c + 2], False)])
            for r in range(2) for c in range(2)
        ]
        second = [
            cmul_add([(a[c], e[r], True), (a[c + 2], e[r + 2], True)])
            for r in range(2) for c in range(2)
        ]
        for k in range(4):
            gp[k, t, :, at] = first[k][0]
            gp[k + 4, t, :, at] = first[k][1]
            gq[k, t, :, at] = second[k][0]
            gq[k + 4, t, :, at] = second[k][1]
        return carry

    lax.fori_loop(0, 16, compute, 0)
    store = pltpu.make_async_copy(res, res_h, out_sem.at[0])
    store.start()

    p_high, p_low = halves(gp[...].reshape(LANES, PAIRS))
    q_high, q_low = halves(gq[...].reshape(LANES, PAIRS))
    nt = (((1,), (1,)), ((), ()))

    def add_up(rows):
        h1, h2 = hot1[rows, :], hot2[rows, :]
        total = lax.dot_general(h1, p_high, nt, preferred_element_type=F32)
        total += lax.dot_general(h1, p_low, nt, preferred_element_type=F32)
        total += lax.dot_general(h2, q_high, nt, preferred_element_type=F32)
        total += lax.dot_general(h2, q_low, nt, preferred_element_type=F32)
        part[rows, :] = total

    theirs = pl.multiple_of((1 - core) * 256, 256)
    mine = pl.multiple_of(core * 256, 256)
    add_up(pl.ds(theirs, 256))
    rc_sends = []
    for k in (1, 2, 3, 0):
        y_to = lax.rem(y + k, NY)
        copy = to_bl(
            part.at[pl.ds(row_of(y_to, 0, 1 - core), 64)], got_core.at[k],
            rcs.at[k], rcr.at[k], other,
        )
        copy.start()
        rc_sends.append(copy)
    add_up(pl.ds(mine, 256))
    ry_sends = []
    for k in (1, 2, 3, 0):
        at = pl.ds(row_of(lax.rem(y + k, NY), 0, core), 64)
        to_bl(part.at[at], got_core.at[k], rcs.at[k], rcr.at[k], other).wait_recv()
        part[at, :] = part[at, :] + got_core[k]
        if k:
            copy = to_bl(part.at[at], got_y.at[k], rys.at[k], ryr.at[k], y_peer[k])
            copy.start()
            ry_sends.append(copy)

    for k in range(2):
        pltpu.make_async_remote_copy(
            src_ref=halo, dst_ref=halo_got.at[k], send_sem=hs.at[k], recv_sem=hr.at[k],
            device_id={"chan": (chan_next, chan_prev)[k]}, device_id_type=MESH,
        ).wait_recv()
    from_prev, from_next = halo_got[0], halo_got[1]
    x = own_x[...]

    def shift(v, by):
        return pltpu.roll(v, by % LANES, 1)

    prev_edge = jnp.concatenate([pltpu.roll(from_prev, 121, 1), pltpu.roll(from_prev, 122, 1)], axis=1)
    next_edge = jnp.concatenate([pltpu.roll(from_next, 7, 1), pltpu.roll(from_next, 6, 1)], axis=1)
    next_weight = jnp.concatenate([pltpu.roll(from_next, 5, 1)] * 2, axis=1)
    is_first, is_last = freq == 0, freq == CHANNELS - 1
    not_low = jnp.where(chan > 0, 1.0, 0.0).astype(F32)
    not_high = jnp.where(chan < n_chan - 1, 1.0, 0.0).astype(F32)

    def slope(w, step):
        square = step * step
        for by in (128, 64, 32):
            square = square + shift(square, by)
        return w * step / jnp.sqrt(square + SMOOTH_EPS)

    grad = slope(
        jnp.where(is_first, weight * not_low, weight), x - jnp.where(is_first, prev_edge, shift(x, 1))
    )
    grad -= slope(
        jnp.where(is_last, next_weight * not_high, shift(weight, -1)),
        jnp.where(is_last, next_edge, shift(x, -1)) - x,
    )
    grad += slope(jnp.where(time > 0, weight, 0.0), x - shift(x, 8))
    grad -= slope(jnp.where(time < TIMES - 1, weight, 0.0), shift(x, -8) - x)
    smooth[...] = x - (STEP * TV_SCALE) * grad

    at = pl.ds(row_of(y, 0, core), 64)
    total = part[at, :]
    for k in range(1, NY):
        to_bl(part.at[at], got_y.at[k], rys.at[k], ryr.at[k], y_peer[k]).wait_recv()
        total = total + got_y[k]
    part[at, :] = total
    rz_sends = []
    for k in range(1, NZ):
        copy = to_bl(
            part.at[pl.ds(row_of(y, lax.rem(z + k, NZ), core), 8)], got_z.at[k],
            rzs.at[k], rzr.at[k], z_peer[k],
        )
        copy.start()
        rz_sends.append(copy)
    total = part[pl.ds(own_row, 8), :]
    for k in range(1, NZ):
        to_bl(part.at[pl.ds(own_row, 8)], got_z.at[k], rzs.at[k], rzr.at[k], z_peer[k]).wait_recv()
        total = total + got_z[k]
    updated = smooth[...] + STEP * total
    upd_ref[...] = jnp.transpose(updated).reshape(8, TIMES, CHANNELS, 8)

    for copy in z_sends + y_sends + c_sends + h_sends + rc_sends + ry_sends + rz_sends:
        copy.wait_send()
    store.wait()


def local(meas, model, imp, tally, one, two, gains, tvw):
    big = (8, TIMES, CHANNELS, PAIRS)
    vmem = pltpu.VMEM
    dma = pltpu.SemaphoreType.DMA
    any_spec = pl.BlockSpec(memory_space=pl.ANY)
    return pl.pallas_call(
        kernel,
        out_shape=(
            jax.ShapeDtypeStruct((8, TIMES, CHANNELS, 8), F32),
            jax.ShapeDtypeStruct(big, F32),
        ),
        in_specs=[any_spec] * 8,
        out_specs=(pl.BlockSpec(memory_space=pltpu.VMEM), any_spec),
        scratch_shapes=[
            vmem(big, F32), vmem(big, F32), vmem((TIMES, CHANNELS, PAIRS), F32),
            vmem((1, PAIRS), jnp.int32), vmem((1, PAIRS), jnp.int32), vmem((1, PAIRS), jnp.int32),
            vmem((8, TIMES, CHANNELS, 8), F32), vmem((CHANNELS, 8), F32),
            vmem((STATIONS, LANES), F32), vmem((STATIONS, PAIRS), BF16), vmem((STATIONS, PAIRS), BF16),
            vmem(big, F32), vmem(big, F32), vmem(big, F32), vmem((STATIONS, LANES), F32),
            vmem((NY, 64, LANES), F32), vmem((NY, 64, LANES), F32), vmem((NZ, 8, LANES), F32),
            vmem((8, 128), F32), vmem((2, 8, 128), F32), vmem((8, LANES), F32), vmem((8, LANES), F32),
            dma((8,)), dma((1,)),
            dma((NZ,)), dma((NZ,)), dma((NY,)), dma((NY,)), dma((NY,)), dma((NY,)), dma((2,)), dma((2,)),
            dma((NY,)), dma((NY,)), dma((NY,)), dma((NY,)), dma((NZ,)), dma((NZ,)),
        ],
        compiler_params=pltpu.CompilerParams(
            collective_id=0, has_side_effects=True, vmem_limit_bytes=40 * 1024 * 1024
        ),
    )(meas, model, imp, tally, one.reshape(1, PAIRS), two.reshape(1, PAIRS), gains, tvw)


def solution(mesh):
    placed = (
        P(None, None, "chan", "bl"),
        P(None, None, "chan", "bl"),
        P(None, "chan", "bl"),
        P("chan", "bl"),
        P("bl"),
        P("bl"),
        P(None, None, "chan", "bl"),
        P("chan", "bl"),
    )
    return jax.shard_map(
        local,
        mesh=mesh,
        in_specs=placed,
        out_specs=(P(None, None, "chan", "bl"), P(None, None, "chan", "bl")),
        check_vma=False,
    )
```

time: 855 us -> 54.2 us (0.06); the launches traced: 844 us -> 53.8 us
  waiting for transfers between devices: 425 us -> 0 us
  blocking collectives: 180 us -> 0 us
  other arithmetic: 141 us -> 0 us
  local copies, waits for them, and re-layouts: 65.5 us -> 8 us
  Pallas kernels: 0 us -> 45.1 us
  starting transfers between devices: 17.6 us -> 0 us
  between operations: 14.4 us -> 0.66 us
    unnamed x2 -> x0, waiting for transfers between devices: 425 us -> none
    all_gather x1 -> x0, blocking collectives: 180 us -> none  [local(): full_gains = lax.all_gather(station_gains, 'bl', axis=3, tiled=True)]
    scatter-add x2 -> x0, other arithmetic: 135 us -> none  [local(): station_table = blank_table.at[:, :, :, antenna_one].add(grad_first).at[:...]
    pallas_call x0 -> x1, Pallas kernels: none -> 45.1 us  [local(): pl.pallas_call(kernel, out_shape=(jax.ShapeDtypeStruct((8, TIMES, CHANNEL...]
    gather x4 -> x0, local copies, waits for them, and re-layouts: 26.9 us -> none  [the longest x2 13.5 us: local(): gain_first = jnp.take(full_gains, antenna_one, axis=3)]
    ppermute x2 -> x0, starting transfers between devices: 17.6 us -> none  [the longest x1 16.3 us: with_halo(): lax.ppermute(tail, axis, [(i, (i + 1) % count) for i in range(ends)])]
    add_any x2 -> x0, local copies, waits for them, and re-layouts: 14.8 us -> none  [the longest x1 7.41 us: adjoint(): matrix[0]]
    unnamed x19 -> x18, local copies, waits for them, and re-layouts: 19.8 us -> 8 us
  transfers between devices with their start and end apart: 3 -> 0, of which waited for: 1 -> 0; matrix products, arithmetic and copies ran while one was open for 24% -> 0% of each run, Pallas kernels for 0% -> 0%
where the time goes in v1:
time: 54.2 us; the launch traced here: 53.8 us
  Pallas kernels  45.1 us (83%)
  local copies, waits for them, and re-layouts  8 us (15%)
  between operations  0.66 us (1%)
    pallas_call x1, Pallas kernels, local(): pl.pallas_call(kernel, out_shape=(jax.ShapeDtypeStruct((8, TIMES, CHANNEL...  45.1 us
    unnamed x18, local copies, waits for them, and re-layouts  8 us

profile of v1, /device:TPU:1, one launch (start us, length us, event | category | flops | bytes accessed | tf_op | source)
XLA Modules:
  0.0 53.8 jit_solution(5722821633695092071)
XLA Ops:
  0.6 0.0 copy-start.5
  0.6 0.7 %copy-done.5 = s32[1,512]{1,0:T(1,128)S(1)} copy-done((s32[1,512]{1,0:T(1,128)S(1)}, s32[1,512]{1,0:T(1,128)}, u32[]{:S(2)}) %copy-start.5) | copy-done | bytes 2072
  1.3 0.0 copy-start
  1.3 1.0 %copy-done = f32[8,4,8,512]{3,2,1,0:T(8,128)S(1)} copy-done((f32[8,4,8,512]{3,2,1,0:T(8,128)S(1)}, f32[8,4,8,512]{3,2,1,0:T(8,128)}, u32[]{:S(2)}) %copy-start) | copy-done | bytes 524312
  2.4 0.0 copy-start.1
  2.4 1.0 %copy-done.1 = f32[8,4,8,512]{3,2,1,0:T(8,128)S(1)} copy-done((f32[8,4,8,512]{3,2,1,0:T(8,128)S(1)}, f32[8,4,8,512]{3,2,1,0:T(8,128)}, u32[]{:S(2)}) %copy-start.1) | copy-done | bytes 524312
  3.4 0.0 copy-start.2
  3.4 0.9 %copy-done.2 = f32[8,4,8,8]{3,2,1,0:T(8,128)S(1)} copy-done((f32[8,4,8,8]{3,2,1,0:T(8,128)S(1)}, f32[8,4,8,8]{3,2,1,0:T(8,128)}, u32[]{:S(2)}) %copy-start.2) | copy-done | bytes 8216
  4.3 0.0 copy-start.3
  4.3 0.8 %copy-done.3 = f32[4,8,512]{2,1,0:T(8,128)S(1)} copy-done((f32[4,8,512]{2,1,0:T(8,128)S(1)}, f32[4,8,512]{2,1,0:T(8,128)}, u32[]{:S(2)}) %copy-start.3) | copy-done | bytes 65560
  5.1 0.0 copy-start.4
  5.1 0.7 %copy-done.4 = f32[8,8]{1,0:T(8,128)S(1)} copy-done((f32[8,8]{1,0:T(8,128)S(1)}, f32[8,8]{1,0:T(8,128)}, u32[]{:S(2)}) %copy-start.4) | copy-done | bytes 280
  5.8 0.0 copy-start.6
  5.8 0.7 %copy-done.6 = s32[512]{0:T(512)S(1)} copy-done((s32[512]{0:T(512)S(1)}, s32[512]{0:T(512)}, u32[]{:S(2)}) %copy-start.6) | copy-done | bytes 2072
  6.5 0.0 copy-start.7
  6.5 0.7 %copy-done.7 = s32[512]{0:T(512)S(1)} copy-done((s32[512]{0:T(512)S(1)}, s32[512]{0:T(512)}, u32[]{:S(2)}) %copy-start.7) | copy-done | bytes 2072
  7.2 45.1 %shard_map.95 = (f32[8,4,8,8]{3,2,1,0:T(8,128)S(1)}, f32[8,4,8,512]{3,2,1,0:T(8,128)S(1)}) custom-call(f32[8,4,8,512]{3,2,1,0:T(8,128)S(1)} %copy-done, f32[8,4,8,512]{3,2,1,0:T(8,128)S(1)} %copy-done.1, f32[4,8,512]{2,1,0:T(8,128)S(1)} %copy-done.3, s32[1,512]{1,0:T(1,128)S(1)} %copy-done.5, s32[1,512]{1,0:T(1,128)S(1)} %bitcast.2, s32[1,512]{1,0:T(1,128)S(1)} %bitcast.3, ...), custom_call_target="tpu_custom_call" | custom-call | tf_op jit(solution)/shard_map/pallas_call | solution.py:342
  52.3 0.7 %copy.12 = f32[8,4,8,8]{3,2,1,0:T(8,128)} copy(f32[8,4,8,8]{3,2,1,0:T(8,128)S(1)} %get-tuple-element.4) | data formatting | bytes 16384
  53.0 0.8 %copy.13 = f32[8,4,8,512]{3,2,1,0:T(8,128)} copy(f32[8,4,8,512]{3,2,1,0:T(8,128)S(1)} %get-tuple-element.5) | data formatting | bytes 1048576
Async XLA Ops:
  0.6 0.7 %copy-start.5 = (s32[1,512]{1,0:T(1,128)S(1)}, s32[1,512]{1,0:T(1,128)}, u32[]{:S(2)}) copy-start(s32[1,512]{1,0:T(1,128)} %tally_h.1) | copy-start | bytes 6148
  1.3 1.0 %copy-start = (f32[8,4,8,512]{3,2,1,0:T(8,128)S(1)}, f32[8,4,8,512]{3,2,1,0:T(8,128)}, u32[]{:S(2)}) copy-start(f32[8,4,8,512]{3,2,1,0:T(8,128)} %meas_h.1) | copy-start | bytes 1572868
  2.4 1.0 %copy-start.1 = (f32[8,4,8,512]{3,2,1,0:T(8,128)S(1)}, f32[8,4,8,512]{3,2,1,0:T(8,128)}, u32[]{:S(2)}) copy-start(f32[8,4,8,512]{3,2,1,0:T(8,128)} %model_h.1) | copy-start | bytes 1572868
  3.4 0.9 %copy-start.2 = (f32[8,4,8,8]{3,2,1,0:T(8,128)S(1)}, f32[8,4,8,8]{3,2,1,0:T(8,128)}, u32[]{:S(2)}) copy-start(f32[8,4,8,8]{3,2,1,0:T(8,128)} %gains_h.1) | copy-start | bytes 24580
  4.3 0.8 %copy-start.3 = (f32[4,8,512]{2,1,0:T(8,128)S(1)}, f32[4,8,512]{2,1,0:T(8,128)}, u32[]{:S(2)}) copy-start(f32[4,8,512]{2,1,0:T(8,128)} %imp_h.1) | copy-start | bytes 196612
  5.1 0.7 %copy-start.4 = (f32[8,8]{1,0:T(8,128)S(1)}, f32[8,8]{1,0:T(8,128)}, u32[]{:S(2)}) copy-start(f32[8,8]{1,0:T(8,128)} %tvw_h.1) | copy-start | bytes 772
  5.8 0.7 %copy-start.6 = (s32[512]{0:T(512)S(1)}, s32[512]{0:T(512)}, u32[]{:S(2)}) copy-start(s32[512]{0:T(512)} %param.12) | copy-start | bytes 6148
  6.5 0.7 %copy-start.7 = (s32[512]{0:T(512)S(1)}, s32[512]{0:T(512)}, u32[]{:S(2)}) copy-start(s32[512]{0:T(512)} %param.13) | copy-start | bytes 6148

commit v2 on v1

v2 whole, which is shorter than its diff:
```python
import jax
import jax.numpy as jnp
from jax import lax
from jax.experimental import pallas as pl
from jax.experimental.pallas import tpu as pltpu
from jax.sharding import PartitionSpec as P

MESH = pl.DeviceIdType.MESH
STATIONS = 512
BASELINES = 32768
TIMES = 4
CHANNELS = 8
PAIRS = 512
LANES = 8 * TIMES * CHANNELS
NY, NZ, NC = 4, 8, 2
SMOOTH_EPS = 0.01
TV_SCALE = 2.0
STEP = 2.0 * STATIONS / BASELINES
F32 = jnp.float32
BF16 = jnp.bfloat16


def cmul_add(terms):
    real, imag = None, None
    for (ar, ai), (br, bi), conj in terms:
        if conj:
            r, i = ar * br + ai * bi, ai * br - ar * bi
        else:
            r, i = ar * br - ai * bi, ar * bi + ai * br
        real = r if real is None else real + r
        imag = i if imag is None else imag + i
    return real, imag


def halves(x):
    high = x.astype(BF16)
    return high, (x - high.astype(F32)).astype(BF16)


def split_index():
    bl = lax.axis_index("bl")
    return lax.div(bl, NZ * NC), lax.rem(lax.div(bl, NC), NZ), lax.rem(bl, NC)


def join_index(y, z, core):
    return (y * NZ + z) * NC + core


def kernel(
    meas_h, model_h, imp_h, tally_h, one_h, two_h, gains_h, tvw_h,
    upd_ref, res,
    meas, model, imp, tally, one, two, gains, tvw,
    table, hot1, hot2, gp, gq, part, got_c, got_y, got_z, halo, halo_got,
    in_sem, zs, zr, ys, yr, cs, cr, hs, hr, rcs, rcr, rys, ryr, rzs, rzr,
):
    chan = lax.axis_index("chan")
    n_chan = lax.axis_size("chan")
    y, z, core = split_index()
    early = lax.rem(chan, 2) == 0
    chan_peers = [lax.rem(chan + 1, n_chan), lax.rem(chan + n_chan - 1, n_chan)]

    def to_bl(src, dst, send, recv, peer):
        return pltpu.make_async_remote_copy(
            src_ref=src, dst_ref=dst, send_sem=send, recv_sem=recv,
            device_id={"bl": peer}, device_id_type=MESH,
        )

    def z_peer(k):
        to = lax.rem(z + k, NZ)
        return join_index(y, to, core), to

    def y_peer(k):
        to = lax.rem(y + k, NY)
        return join_index(to, z, core), to

    other = join_index(y, z, 1 - core)

    loads = [
        pltpu.make_async_copy(src, dst, in_sem.at[i])
        for i, (src, dst) in enumerate(
            [(gains_h, gains), (one_h, one), (two_h, two), (tvw_h, tvw), (tally_h, tally),
             (imp_h, imp), (meas_h, meas), (model_h, model)]
        )
    ]
    loads[0].start()
    barrier = pltpu.get_barrier_semaphore()
    for peer in [z_peer(k)[0] for k in range(1, NZ)] + [y_peer(k)[0] for k in range(1, NY)] + [other]:
        pl.semaphore_signal(barrier, inc=1, device_id={"bl": peer}, device_id_type=MESH)

    @pl.when(early)
    def _():
        for peer in chan_peers:
            pl.semaphore_signal(barrier, inc=1, device_id={"chan": peer}, device_id_type=MESH)

    for load in loads[1:]:
        load.start()

    loads[0].wait()
    own = jnp.transpose(gains[...].reshape(LANES, 8))
    table[z, core, y] = own
    pl.semaphore_wait(barrier, 11 + 2 * lax.rem(chan, 2))

    for k in range(1, NZ):
        piece = table.at[z, core, y]
        to_bl(piece, piece, zs.at[0], zr.at[z], z_peer(k)[0]).start()

    def pass_on(v):
        piece = table.at[v, core, y]
        for k in (2, 1, 3):
            to_bl(piece, piece, ys.at[0], yr.at[v], y_peer(k)[0]).start()

    pass_on(z)

    loads[3].wait()
    lane = lax.broadcasted_iota(jnp.int32, (8, LANES), 1)
    freq, time = lane & 7, lax.shift_right_logical(lane, 3) & 3
    weight = jnp.transpose(
        jnp.broadcast_to(tvw[...][None], (8 * TIMES, CHANNELS, 8)).reshape(LANES, 8)
    )
    low, high = own[:, :128], own[:, 128:]
    freq_h = freq[:, :128]
    halo[...] = jnp.where(
        freq_h == 0, low,
        jnp.where(
            freq_h == 1, pltpu.roll(high, 1, 1),
            jnp.where(
                freq_h == 7, low,
                jnp.where(freq_h == 6, pltpu.roll(high, 127, 1), pltpu.roll(weight[:, :128], 2, 1)),
            ),
        ),
    )
    edges = [
        pltpu.make_async_remote_copy(
            src_ref=halo, dst_ref=halo_got.at[k], send_sem=hs.at[k], recv_sem=hr.at[k],
            device_id={"chan": peer}, device_id_type=MESH,
        )
        for k, peer in enumerate(chan_peers)
    ]

    @pl.when(jnp.logical_not(early))
    def _():
        for edge in edges:
            edge.start()

    loads[1].wait()
    loads[2].wait()

    def to_row(ant):
        return (
            (lax.shift_right_logical(ant, 4) & 7) * 64 + (lax.shift_right_logical(ant, 3) & 1) * 32
            + lax.shift_right_logical(ant, 7) * 8 + (ant & 7)
        )

    row1, row2 = to_row(one[...]), to_row(two[...])

    def hot_body(i, carry):
        base = pl.multiple_of(i * 32, 32)
        index = lax.broadcasted_iota(jnp.int32, (32, PAIRS), 0) + base
        hot1[pl.ds(base, 32), :] = jnp.where(index == row1, 1.0, 0.0).astype(BF16)
        hot2[pl.ds(base, 32), :] = jnp.where(index == row2, 1.0, 0.0).astype(BF16)
        return carry

    lax.fori_loop(0, 16, hot_body, 0)

    loads[4].wait()
    loads[5].wait()
    keep = lax.broadcasted_iota(jnp.int32, (CHANNELS, PAIRS), 0) < CHANNELS - tally[...]
    for t in range(TIMES):
        imp[t] = jnp.where(keep, imp[t], 0.0)
    loads[6].wait()
    loads[7].wait()

    def take_in(v, carry):
        @pl.when(v != z)
        def _():
            piece = table.at[v, core, y]
            to_bl(piece, piece, zs.at[0], zr.at[v], z_peer(1)[0]).wait_recv()
            pass_on(v)

        return carry

    def share(v, carry):
        three = table.at[v, core, pl.ds(0, 3)]
        to_bl(three, three, ys.at[0], yr.at[v], other).wait_recv()
        four = table.at[v, core]
        to_bl(four, four, cs.at[0], cr.at[v], other).start()
        return carry

    def pick(half, first):
        def arrived(v, carry):
            four = table.at[v, 1 - core]
            to_bl(four, four, cs.at[0], cr.at[v], other).wait_recv()
            return carry

        lax.fori_loop(half * 4, half * 4 + 4, arrived, 0)
        flipped = jnp.transpose(table[pl.ds(half * 4, 4)].reshape(256, LANES))
        g_high, g_low = halves(flipped)
        rows = pl.ds(half * 256, 256)
        for hot, dst in ((hot1, gp), (hot2, gq)):
            picked = jnp.dot(g_high, hot[rows, :], preferred_element_type=F32) + jnp.dot(
                g_low, hot[rows, :], preferred_element_type=F32
            )
            picked = picked.reshape(8, TIMES, CHANNELS, PAIRS)
            dst[...] = picked if first else dst[...] + picked

    lax.fori_loop(0, 8, take_in, 0)
    lax.fori_loop(0, 8, share, 0)
    pick(0, True)
    pick(1, False)

    def compute(i, carry):
        t = lax.div(i, 4)
        at = pl.ds(pl.multiple_of(lax.rem(i, 4) * 128, 128), 128)

        def matrix(ref):
            return [(ref[c, t, :, at], ref[c + 4, t, :, at]) for c in range(4)]

        jp, jq, m, d = matrix(gp), matrix(gq), matrix(model), matrix(meas)
        w = imp[t, :, at]
        a = [
            cmul_add([(jp[2 * r], m[c], False), (jp[2 * r + 1], m[c + 2], False)])
            for r in range(2) for c in range(2)
        ]
        v = [
            cmul_add([(a[2 * r], jq[2 * c], True), (a[2 * r + 1], jq[2 * c + 1], True)])
            for r in range(2) for c in range(2)
        ]
        e = [(w * (d[k][0] - v[k][0]), w * (d[k][1] - v[k][1])) for k in range(4)]
        for k in range(4):
            res[k, t, :, at] = e[k][0]
            res[k + 4, t, :, at] = e[k][1]
        b = [
            cmul_add([(jq[2 * r], m[2 * c], True), (jq[2 * r + 1], m[2 * c + 1], True)])
            for r in range(2) for c in range(2)
        ]
        first = [
            cmul_add([(e[2 * r], b[c], False), (e[2 * r + 1], b[c + 2], False)])
            for r in range(2) for c in range(2)
        ]
        second = [
            cmul_add([(a[c], e[r], True), (a[c + 2], e[r + 2], True)])
            for r in range(2) for c in range(2)
        ]
        for k in range(4):
            gp[k, t, :, at] = first[k][0]
            gp[k + 4, t, :, at] = first[k][1]
            gq[k, t, :, at] = second[k][0]
            gq[k + 4, t, :, at] = second[k][1]
        return carry

    lax.fori_loop(0, 16, compute, 0)

    p_high, p_low = halves(gp[...].reshape(LANES, PAIRS))
    q_high, q_low = halves(gq[...].reshape(LANES, PAIRS))
    nt = (((1,), (1,)), ((), ()))

    def add_up(v, count):
        rows = pl.ds(v * 64, count * 64)
        h1, h2 = hot1[rows, :], hot2[rows, :]
        total = lax.dot_general(h1, p_high, nt, preferred_element_type=F32)
        total += lax.dot_general(h1, p_low, nt, preferred_element_type=F32)
        total += lax.dot_general(h2, q_high, nt, preferred_element_type=F32)
        total += lax.dot_general(h2, q_low, nt, preferred_element_type=F32)
        part[pl.ds(v, count)] = total.reshape(count, NC, NY, 8, LANES)

    def hand_over(v, carry):
        to_bl(part.at[v, 1 - core], got_c.at[v], rcs.at[0], rcr.at[v], other).start()
        return carry

    def along_y(v, carry):
        got = got_c.at[v]
        to_bl(got, got, rcs.at[0], rcr.at[v], other).wait_recv()
        part[v, core] = part[v, core] + got_c[v]
        for k in (2, 1, 3):
            peer, to = y_peer(k)
            to_bl(part.at[v, core, to], got_y.at[v, k - 1], rys.at[0], ryr.at[v], peer).start()
        return carry

    def along_z(v, carry):
        got = got_y.at[v]
        to_bl(got, got, rys.at[0], ryr.at[v], other).wait_recv()
        part[v, core, y] = part[v, core, y] + got_y[v, 0] + (got_y[v, 1] + got_y[v, 2])

        @pl.when(v != z)
        def _():
            to_bl(
                part.at[v, core, y], got_z.at[z], rzs.at[0], rzr.at[0], join_index(y, v, core)
            ).start()

        return carry

    add_up(0, 1)
    hand_over(0, 0)
    add_up(1, 7)
    lax.fori_loop(1, 8, hand_over, 0)
    lax.fori_loop(0, 8, along_y, 0)
    lax.fori_loop(0, 8, along_z, 0)
    got_z[z] = part[z, core, y]

    for edge in edges:
        edge.wait_recv()

    @pl.when(early)
    def _():
        for edge in edges:
            edge.start()

    from_prev, from_next = halo_got[0], halo_got[1]
    x = own

    def shift(v, by):
        return pltpu.roll(v, by % LANES, 1)

    prev_edge = jnp.concatenate([pltpu.roll(from_prev, 121, 1), pltpu.roll(from_prev, 122, 1)], axis=1)
    next_edge = jnp.concatenate([pltpu.roll(from_next, 7, 1), pltpu.roll(from_next, 6, 1)], axis=1)
    next_weight = jnp.concatenate([pltpu.roll(from_next, 5, 1)] * 2, axis=1)
    is_first, is_last = freq == 0, freq == CHANNELS - 1
    not_low = jnp.where(chan > 0, 1.0, 0.0).astype(F32)
    not_high = jnp.where(chan < n_chan - 1, 1.0, 0.0).astype(F32)

    def slope(w, step):
        square = step * step
        for by in (128, 64, 32):
            square = square + shift(square, by)
        return w * step / jnp.sqrt(square + SMOOTH_EPS)

    grad = slope(
        jnp.where(is_first, weight * not_low, weight), x - jnp.where(is_first, prev_edge, shift(x, 1))
    )
    grad -= slope(
        jnp.where(is_last, next_weight * not_high, shift(weight, -1)),
        jnp.where(is_last, next_edge, shift(x, -1)) - x,
    )
    grad += slope(jnp.where(time > 0, weight, 0.0), x - shift(x, 8))
    grad -= slope(jnp.where(time < TIMES - 1, weight, 0.0), shift(x, -8) - x)
    updated = x - (STEP * TV_SCALE) * grad

    rows = got_z.at[pl.ds(0, NZ - 1)]
    to_bl(rows, rows, rzs.at[0], rzr.at[0], z_peer(1)[0]).wait_recv()
    total = got_z[0]
    for v in range(1, NZ):
        total = total + got_z[v]
    updated = updated + STEP * total
    upd_ref[...] = jnp.transpose(updated).reshape(8, TIMES, CHANNELS, 8)

    for edge in edges:
        edge.wait_send()
    to_bl(rows, rows, zs.at[0], rzr.at[0], other).wait_send()
    to_bl(rows, rows, rzs.at[0], rzr.at[0], other).wait_send()
    half = part.at[pl.ds(0, NZ), 0]
    to_bl(half, half, cs.at[0], rzr.at[0], other).wait_send()
    to_bl(half, half, rcs.at[0], rzr.at[0], other).wait_send()
    to_bl(got_y, got_y, ys.at[0], rzr.at[0], other).wait_send()
    to_bl(got_y, got_y, rys.at[0], rzr.at[0], other).wait_send()


def local(meas, model, imp, tally, one, two, gains, tvw):
    big = (8, TIMES, CHANNELS, PAIRS)
    vmem = pltpu.VMEM
    dma = pltpu.SemaphoreType.DMA
    any_spec = pl.BlockSpec(memory_space=pl.ANY)
    vmem_spec = pl.BlockSpec(memory_space=pltpu.VMEM)
    return pl.pallas_call(
        kernel,
        out_shape=(vmem((8, TIMES, CHANNELS, 8), F32), vmem(big, F32)),
        in_specs=[any_spec] * 8,
        out_specs=(vmem_spec, vmem_spec),
        scratch_shapes=[
            vmem(big, F32), vmem(big, F32), vmem((TIMES, CHANNELS, PAIRS), F32),
            vmem((1, PAIRS), jnp.int32), vmem((1, PAIRS), jnp.int32), vmem((1, PAIRS), jnp.int32),
            vmem((8, TIMES, CHANNELS, 8), F32), vmem((CHANNELS, 8), F32),
            vmem((NZ, NC, NY, 8, LANES), F32), vmem((STATIONS, PAIRS), BF16), vmem((STATIONS, PAIRS), BF16),
            vmem(big, F32), vmem(big, F32), vmem((NZ, NC, NY, 8, LANES), F32),
            vmem((NZ, NY, 8, LANES), F32), vmem((NZ, NY - 1, 8, LANES), F32), vmem((NZ, 8, LANES), F32),
            vmem((8, 128), F32), vmem((2, 8, 128), F32),
            dma((8,)), dma((1,)), dma((NZ,)), dma((1,)), dma((NZ,)), dma((1,)), dma((NZ,)), dma((2,)), dma((2,)),
            dma((1,)), dma((NZ,)), dma((1,)), dma((NZ,)), dma((1,)), dma((1,)),
        ],
        compiler_params=pltpu.CompilerParams(
            collective_id=0, has_side_effects=True, vmem_limit_bytes=58 * 1024 * 1024
        ),
    )(meas, model, imp, tally, one.reshape(1, PAIRS), two.reshape(1, PAIRS), gains, tvw)


def solution(mesh):
    placed = (
        P(None, None, "chan", "bl"),
        P(None, None, "chan", "bl"),
        P(None, "chan", "bl"),
        P("chan", "bl"),
        P("bl"),
        P("bl"),
        P(None, None, "chan", "bl"),
        P("chan", "bl"),
    )
    return jax.shard_map(
        local,
        mesh=mesh,
        in_specs=placed,
        out_specs=(P(None, None, "chan", "bl"), P(None, None, "chan", "bl")),
        check_vma=False,
    )
```

time: 54.2 us -> 40.2 us (0.74)
  Pallas kernels: 45.1 us -> 37.5 us
  local copies, waits for them, and re-layouts: 8 us -> 1.45 us
    pallas_call x1, Pallas kernels: 45.1 us -> 37.5 us  [local(): pl.pallas_call(kernel, out_shape=(vmem((8, TIMES, CHANNELS, 8), F32), vme...]
    unnamed x18 -> x2, local copies, waits for them, and re-layouts: 8 us -> 1.45 us
where the time goes in v2:
time: 40.2 us; the launch traced here: 39.6 us
  Pallas kernels  37.5 us (93%)
  local copies, waits for them, and re-layouts  1.45 us (4%)
  between operations  0.64 us (2%)
    pallas_call x1, Pallas kernels, local(): pl.pallas_call(kernel, out_shape=(vmem((8, TIMES, CHANNELS, 8), F32), vme...  37.5 us
    unnamed x2, local copies, waits for them, and re-layouts  1.45 us

profile of v2, /device:TPU:1, one launch (start us, length us, event | category | flops | bytes accessed | tf_op | source)
XLA Modules:
  0.0 39.6 jit_solution(12664615915559378397)
XLA Ops:
  0.6 37.5 %shard_map.95 = (f32[8,4,8,8]{3,2,1,0:T(8,128)S(1)}, f32[8,4,8,512]{3,2,1,0:T(8,128)S(1)}) custom-call(f32[8,4,8,512]{3,2,1,0:T(8,128)} %meas_h.1, f32[8,4,8,512]{3,2,1,0:T(8,128)} %model_h.1, f32[4,8,512]{2,1,0:T(8,128)} %imp_h.1, s32[1,512]{1,0:T(1,128)} %tally_h.1, s32[1,512]{1,0:T(1,128)} %bitcast.2, s32[1,512]{1,0:T(1,128)} %bitcast.3, ...), custom_call_target="tpu_custom_call" | custom-call | tf_op jit(solution)/shard_map/pallas_call | solution.py:363
  38.2 0.7 %copy.12 = f32[8,4,8,8]{3,2,1,0:T(8,128)} copy(f32[8,4,8,8]{3,2,1,0:T(8,128)S(1)} %get-tuple-element.2) | data formatting | bytes 16384
  38.8 0.8 %copy.13 = f32[8,4,8,512]{3,2,1,0:T(8,128)} copy(f32[8,4,8,512]{3,2,1,0:T(8,128)S(1)} %get-tuple-element.3) | data formatting | bytes 1048576

commit v3 on v2

--- a/solution.py
+++ b/solution.py
@@ -1,3 +1,5 @@
+import functools
+
 import jax
 import jax.numpy as jnp
 from jax import lax
@@ -13,6 +15,8 @@
 PAIRS = 512
 LANES = 8 * TIMES * CHANNELS
 NY, NZ, NC = 4, 8, 2
+HALF = NZ // 2
+DIRECT = 2
 SMOOTH_EPS = 0.01
 TV_SCALE = 2.0
 STEP = 2.0 * STATIONS / BASELINES
@@ -50,13 +54,15 @@
     meas_h, model_h, imp_h, tally_h, one_h, two_h, gains_h, tvw_h,
     upd_ref, res,
     meas, model, imp, tally, one, two, gains, tvw,
-    table, hot1, hot2, gp, gq, part, got_c, got_y, got_z, halo, halo_got,
-    in_sem, zs, zr, ys, yr, cs, cr, hs, hr, rcs, rcr, rys, ryr, rzs, rzr,
+    table, hot1, hot2, gp, gq, part, got_0, got_c, got_y, got_z, halo, halo_got,
+    in_sem, zs, zr, ys, yr, cs, cr, hs, hr, r0s, r0r, rcs, rcr, rys, ryr, rzs, rzr,
+    ready_z, ready_y, ready_c,
 ):
     chan = lax.axis_index("chan")
     n_chan = lax.axis_size("chan")
+    odd = lax.rem(chan, 2)
     y, z, core = split_index()
-    early = lax.rem(chan, 2) == 0
+    early = odd == 0
     chan_peers = [lax.rem(chan + 1, n_chan), lax.rem(chan + n_chan - 1, n_chan)]
 
     def to_bl(src, dst, send, recv, peer):
@@ -65,9 +71,8 @@
             device_id={"bl": peer}, device_id_type=MESH,
         )
 
-    def z_peer(k):
-        to = lax.rem(z + k, NZ)
-        return join_index(y, to, core), to
+    def z_peer(to):
+        return join_index(y, to, core)
 
     def y_peer(k):
         to = lax.rem(y + k, NY)
@@ -84,32 +89,69 @@
     ]
     loads[0].start()
     barrier = pltpu.get_barrier_semaphore()
-    for peer in [z_peer(k)[0] for k in range(1, NZ)] + [y_peer(k)[0] for k in range(1, NY)] + [other]:
-        pl.semaphore_signal(barrier, inc=1, device_id={"bl": peer}, device_id_type=MESH)
+
+    def rank_of(to):
+        return lax.rem(to, 2) * 2 + lax.div(to, 2)
+
+    rank = rank_of(y)
+    upper = lax.div(z, HALF)
+
+    def announce(to, carry):
+        pl.semaphore_signal(barrier, inc=1, device_id={"bl": z_peer(to)}, device_id_type=MESH)
+        return carry
+
+    lax.fori_loop(z + 1, NZ, announce, 0)
+    for k in range(1, NY):
+        peer, to = y_peer(k)
+
+        @pl.when(rank_of(to) > rank)
+        def _():
+            pl.semaphore_signal(barrier, inc=1, device_id={"bl": peer}, device_id_type=MESH)
+
+    @pl.when(core == 0)
+    def _():
+        pl.semaphore_signal(barrier, inc=1, device_id={"bl": other}, device_id_type=MESH)
 
     @pl.when(early)
     def _():
         for peer in chan_peers:
             pl.semaphore_signal(barrier, inc=1, device_id={"chan": peer}, device_id_type=MESH)
 
-    for load in loads[1:]:
-        load.start()
+    earlier = z + rank + core + 2 * odd
+
+    @pl.when(earlier > 0)
+    def _():
+        pl.semaphore_wait(barrier, earlier)
+
+    def tell_z(to, carry):
+        pl.semaphore_signal(ready_z.at[z], inc=1, device_id={"bl": z_peer(to)}, device_id_type=MESH)
+        return carry
+
+    lax.fori_loop(upper * (HALF - 1), z, tell_z, 0)
+    for k in range(1, NY):
+        peer, to = y_peer(k)
+
+        @pl.when(rank_of(to) < rank)
+        def _():
+            pl.semaphore_signal(ready_y, inc=1, device_id={"bl": peer}, device_id_type=MESH)
+
+    @pl.when(core == 1)
+    def _():
+        pl.semaphore_signal(ready_c, inc=1, device_id={"bl": other}, device_id_type=MESH)
 
     loads[0].wait()
     own = jnp.transpose(gains[...].reshape(LANES, 8))
     table[z, core, y] = own
-    pl.semaphore_wait(barrier, 11 + 2 * lax.rem(chan, 2))
-
-    for k in range(1, NZ):
-        piece = table.at[z, core, y]
-        to_bl(piece, piece, zs.at[0], zr.at[z], z_peer(k)[0]).start()
-
-    def pass_on(v):
-        piece = table.at[v, core, y]
-        for k in (2, 1, 3):
-            to_bl(piece, piece, ys.at[0], yr.at[v], y_peer(k)[0]).start()
-
-    pass_on(z)
+
+    mine = table.at[z, core, y]
+
+    def send_down(to, carry):
+        to_bl(mine, mine, zs.at[0], zr.at[z], z_peer(to)).start()
+        return carry
+
+    lax.fori_loop(0, z, send_down, 0)
+    for load in loads[1:]:
+        load.start()
 
     loads[3].wait()
     lane = lax.broadcasted_iota(jnp.int32, (8, LANES), 1)
@@ -170,32 +212,39 @@
     loads[6].wait()
     loads[7].wait()
 
-    def take_in(v, carry):
-        @pl.when(v != z)
-        def _():
-            piece = table.at[v, core, y]
-            to_bl(piece, piece, zs.at[0], zr.at[v], z_peer(1)[0]).wait_recv()
-            pass_on(v)
-
-        return carry
-
-    def share(v, carry):
-        three = table.at[v, core, pl.ds(0, 3)]
-        to_bl(three, three, ys.at[0], yr.at[v], other).wait_recv()
-        four = table.at[v, core]
-        to_bl(four, four, cs.at[0], cr.at[v], other).start()
-        return carry
+    def pieces(v, count):
+        return table.at[v, core, y] if count == 1 else table.at[pl.ds(v, count), core, y]
+
+    def send_up(to, v, count):
+        pl.semaphore_wait(ready_z.at[to], 1)
+        rows = pieces(v, count)
+        to_bl(rows, rows, zs.at[1], zr.at[v], z_peer(to)).start()
+
+    def wait_for(v, count=1):
+        rows = pieces(v, count)
+        to_bl(rows, rows, zs.at[1], zr.at[v], other).wait_recv()
+
+    def pass_on(v, count=1):
+        rows = pieces(v, count)
+        for k in (2, 1, 3):
+            to_bl(rows, rows, ys.at[0], yr.at[v // HALF], y_peer(k)[0]).start()
+
+    def take_in(v, count=1):
+        wait_for(v, count)
+        pass_on(v, count)
+
+    def share(half):
+        three = table.at[pl.ds(half * HALF, HALF), core, pl.ds(0, 3)]
+        to_bl(three, three, ys.at[0], yr.at[half], other).wait_recv()
+        four = table.at[pl.ds(half * HALF, HALF), core]
+        to_bl(four, four, cs.at[0], cr.at[half], other).start()
 
     def pick(half, first):
-        def arrived(v, carry):
-            four = table.at[v, 1 - core]
-            to_bl(four, four, cs.at[0], cr.at[v], other).wait_recv()
-            return carry
-
-        lax.fori_loop(half * 4, half * 4 + 4, arrived, 0)
-        flipped = jnp.transpose(table[pl.ds(half * 4, 4)].reshape(256, LANES))
+        four = table.at[pl.ds(half * HALF, HALF), 1 - core]
+        to_bl(four, four, cs.at[0], cr.at[half], other).wait_recv()
+        flipped = jnp.transpose(table[pl.ds(half * HALF, HALF)].reshape(256, LANES))
         g_high, g_low = halves(flipped)
-        rows = pl.ds(half * 256, 256)
+        rows = pl.ds(pl.multiple_of(half * 256, 256), 256)
         for hot, dst in ((hot1, gp), (hot2, gq)):
             picked = jnp.dot(g_high, hot[rows, :], preferred_element_type=F32) + jnp.dot(
                 g_low, hot[rows, :], preferred_element_type=F32
@@ -203,10 +252,41 @@
             picked = picked.reshape(8, TIMES, CHANNELS, PAIRS)
             dst[...] = picked if first else dst[...] + picked
 
-    lax.fori_loop(0, 8, take_in, 0)
-    lax.fori_loop(0, 8, share, 0)
-    pick(0, True)
-    pick(1, False)
+    def line(at):
+        for to in range(at + 1, at // HALF * HALF + HALF):
+            send_up(to, at, 1)
+
+        @pl.when(rank < NY - 1)
+        def _():
+            pl.semaphore_wait(ready_y, NY - 1 - rank)
+
+        pass_on(at)
+        if at < HALF:
+            for v in range(HALF):
+                if v != at:
+                    take_in(v)
+            if at == HALF - 1:
+                for to in (4, 7, 6, 5):
+                    send_up(to, 0, HALF)
+            for v in range(HALF, NZ):
+                take_in(v)
+        else:
+            for v in range(HALF, NZ):
+                if v != at:
+                    take_in(v)
+            take_in(0, HALF)
+
+    for at in range(NZ):
+        pl.when(z == at)(functools.partial(line, at))
+
+    @pl.when(core == 0)
+    def _():
+        pl.semaphore_wait(ready_c, 1)
+
+    share(upper)
+    share(1 - upper)
+    pick(upper, True)
+    pick(1 - upper, False)
 
     def compute(i, carry):
         t = lax.div(i, 4)
@@ -276,25 +356,38 @@
             to_bl(part.at[v, core, to], got_y.at[v, k - 1], rys.at[0], ryr.at[v], peer).start()
         return carry
 
+    def send_on(v):
+        @pl.when(v != z)
+        def _():
+            to_bl(part.at[v, core, y], got_z.at[z], rzs.at[0], rzr.at[0], z_peer(v)).start()
+
     def along_z(v, carry):
         got = got_y.at[v]
         to_bl(got, got, rys.at[0], ryr.at[v], other).wait_recv()
         part[v, core, y] = part[v, core, y] + got_y[v, 0] + (got_y[v, 1] + got_y[v, 2])
-
-        @pl.when(v != z)
-        def _():
+        send_on(v)
+        return carry
+
+    add_up(0, DIRECT)
+    for v in range(DIRECT):
+        for slot, (dy, dc) in enumerate(((2, 0), (2, 1), (1, 0), (1, 1), (3, 0), (3, 1), (0, 1))):
+            to_y, to_core = lax.rem(y + dy, NY), lax.rem(core + dc, NC)
             to_bl(
-                part.at[v, core, y], got_z.at[z], rzs.at[0], rzr.at[0], join_index(y, v, core)
+                part.at[v, to_core, to_y], got_0.at[v, slot], r0s.at[0], r0r.at[v],
+                join_index(to_y, z, to_core),
             ).start()
-
-        return carry
-
-    add_up(0, 1)
-    hand_over(0, 0)
-    add_up(1, 7)
-    lax.fori_loop(1, 8, hand_over, 0)
-    lax.fori_loop(0, 8, along_y, 0)
-    lax.fori_loop(0, 8, along_z, 0)
+    add_up(DIRECT, NZ - DIRECT)
+    lax.fori_loop(DIRECT, NZ, hand_over, 0)
+    lax.fori_loop(DIRECT, NZ, along_y, 0)
+    for v in range(DIRECT):
+        got = got_0.at[v]
+        to_bl(got, got, r0s.at[0], r0r.at[v], other).wait_recv()
+        total = part[v, core, y]
+        for slot in range(7):
+            total = total + got_0[v, slot]
+        part[v, core, y] = total
+        send_on(v)
+    lax.fori_loop(DIRECT, NZ, along_z, 0)
     got_z[z] = part[z, core, y]
 
     for edge in edges:
@@ -336,7 +429,7 @@
     updated = x - (STEP * TV_SCALE) * grad
 
     rows = got_z.at[pl.ds(0, NZ - 1)]
-    to_bl(rows, rows, rzs.at[0], rzr.at[0], z_peer(1)[0]).wait_recv()
+    to_bl(rows, rows, rzs.at[0], rzr.at[0], other).wait_recv()
     total = got_z[0]
     for v in range(1, NZ):
         total = total + got_z[v]
@@ -345,19 +438,32 @@
 
     for edge in edges:
         edge.wait_send()
-    to_bl(rows, rows, zs.at[0], rzr.at[0], other).wait_send()
+
+    def left(at):
+        for sem, count in ((0, at), (1, (3, 2, 1, 16, 3, 2, 1, 0)[at])):
+            if count:
+                sent = part.at[pl.ds(0, count), 0, 0] if count <= NZ else part.at[pl.ds(0, count // NY), 0]
+                to_bl(sent, sent, zs.at[sem], rzr.at[0], other).wait_send()
+
+    for at in range(NZ):
+        pl.when(z == at)(functools.partial(left, at))
+
     to_bl(rows, rows, rzs.at[0], rzr.at[0], other).wait_send()
     half = part.at[pl.ds(0, NZ), 0]
     to_bl(half, half, cs.at[0], rzr.at[0], other).wait_send()
-    to_bl(half, half, rcs.at[0], rzr.at[0], other).wait_send()
+    seven = part.at[pl.ds(0, NZ - DIRECT), 0]
+    to_bl(seven, seven, rcs.at[0], rzr.at[0], other).wait_send()
+    to_bl(got_0, got_0, r0s.at[0], rzr.at[0], other).wait_send()
     to_bl(got_y, got_y, ys.at[0], rzr.at[0], other).wait_send()
-    to_bl(got_y, got_y, rys.at[0], rzr.at[0], other).wait_send()
+    most = got_y.at[pl.ds(0, NZ - DIRECT)]
+    to_bl(most, most, rys.at[0], rzr.at[0], other).wait_send()
 
 
 def local(meas, model, imp, tally, one, two, gains, tvw):
     big = (8, TIMES, CHANNELS, PAIRS)
     vmem = pltpu.VMEM
     dma = pltpu.SemaphoreType.DMA
+    flag = pltpu.SemaphoreType.REGULAR
     any_spec = pl.BlockSpec(memory_space=pl.ANY)
     vmem_spec = pl.BlockSpec(memory_space=pltpu.VMEM)
     return pl.pallas_call(
@@ -371,10 +477,11 @@
             vmem((8, TIMES, CHANNELS, 8), F32), vmem((CHANNELS, 8), F32),
             vmem((NZ, NC, NY, 8, LANES), F32), vmem((STATIONS, PAIRS), BF16), vmem((STATIONS, PAIRS), BF16),
             vmem(big, F32), vmem(big, F32), vmem((NZ, NC, NY, 8, LANES), F32),
-            vmem((NZ, NY, 8, LANES), F32), vmem((NZ, NY - 1, 8, LANES), F32), vmem((NZ, 8, LANES), F32),
+            vmem((DIRECT, 7, 8, LANES), F32), vmem((NZ, NY, 8, LANES), F32), vmem((NZ, NY - 1, 8, LANES), F32), vmem((NZ, 8, LANES), F32),
             vmem((8, 128), F32), vmem((2, 8, 128), F32),
-            dma((8,)), dma((1,)), dma((NZ,)), dma((1,)), dma((NZ,)), dma((1,)), dma((NZ,)), dma((2,)), dma((2,)),
-            dma((1,)), dma((NZ,)), dma((1,)), dma((NZ,)), dma((1,)), dma((1,)),
+            dma((8,)), dma((2,)), dma((NZ,)), dma((1,)), dma((2,)), dma((1,)), dma((2,)), dma((2,)), dma((2,)),
+            dma((1,)), dma((DIRECT,)), dma((1,)), dma((NZ,)), dma((1,)), dma((NZ,)), dma((1,)), dma((1,)),
+            flag((NZ,)), flag, flag,
         ],
         compiler_params=pltpu.CompilerParams(
             collective_id=0, has_side_effects=True, vmem_limit_bytes=58 * 1024 * 1024

time: 40.2 us -> 37.6 us (0.935); the launches traced: 39.6 us -> 37.5 us
  Pallas kernels: 37.5 us -> 35.4 us
    pallas_call x1, Pallas kernels: 37.5 us -> 35.4 us  [local(): pl.pallas_call(kernel, out_shape=(vmem((8, TIMES, CHANNELS, 8), F32), vme...]
where the time goes in v3:
time: 37.6 us; the launch traced here: 37.5 us
  Pallas kernels  35.4 us (94%)
  local copies, waits for them, and re-layouts  1.45 us (4%)
  between operations  0.64 us (2%)
    pallas_call x1, Pallas kernels, local(): pl.pallas_call(kernel, out_shape=(vmem((8, TIMES, CHANNELS, 8), F32), vme...  35.4 us
    unnamed x2, local copies, waits for them, and re-layouts  1.45 us

profile of v3, /device:TPU:1, one launch (start us, length us, event | category | flops | bytes accessed | tf_op | source)
XLA Modules:
  0.0 37.5 jit_solution(5767917992599778933)
XLA Ops:
  0.6 35.4 %shard_map.95 = (f32[8,4,8,8]{3,2,1,0:T(8,128)S(1)}, f32[8,4,8,512]{3,2,1,0:T(8,128)S(1)}) custom-call(f32[8,4,8,512]{3,2,1,0:T(8,128)} %meas_h.1, f32[8,4,8,512]{3,2,1,0:T(8,128)} %model_h.1, f32[4,8,512]{2,1,0:T(8,128)} %imp_h.1, s32[1,512]{1,0:T(1,128)} %tally_h.1, s32[1,512]{1,0:T(1,128)} %bitcast.2, s32[1,512]{1,0:T(1,128)} %bitcast.3, ...), custom_call_target="tpu_custom_call" | custom-call | tf_op jit(solution)/shard_map/pallas_call | solution.py:469
  36.0 0.7 %copy.12 = f32[8,4,8,8]{3,2,1,0:T(8,128)} copy(f32[8,4,8,8]{3,2,1,0:T(8,128)S(1)} %get-tuple-element.2) | data formatting | bytes 16384
  36.7 0.8 %copy.13 = f32[8,4,8,512]{3,2,1,0:T(8,128)} copy(f32[8,4,8,512]{3,2,1,0:T(8,128)S(1)} %get-tuple-element.3) | data formatting | bytes 1048576

commit v4 on v3

--- a/solution.py
+++ b/solution.py
@@ -56,7 +56,7 @@
     meas, model, imp, tally, one, two, gains, tvw,
     table, hot1, hot2, gp, gq, part, got_0, got_c, got_y, got_z, halo, halo_got,
     in_sem, zs, zr, ys, yr, cs, cr, hs, hr, r0s, r0r, rcs, rcr, rys, ryr, rzs, rzr,
-    ready_z, ready_y, ready_c,
+    ready_z, ready_y, ready_c, hub,
 ):
     chan = lax.axis_index("chan")
     n_chan = lax.axis_size("chan")
@@ -90,25 +90,27 @@
     loads[0].start()
     barrier = pltpu.get_barrier_semaphore()
 
-    def rank_of(to):
-        return lax.rem(to, 2) * 2 + lax.div(to, 2)
-
-    rank = rank_of(y)
+    second = lax.rem(y + core, 2)
     upper = lax.div(z, HALF)
+    beside = [y_peer(1)[0], y_peer(3)[0], other]
+
+    def tell_beside(sem):
+        for peer in beside:
+            pl.semaphore_signal(sem, inc=1, device_id={"bl": peer}, device_id_type=MESH)
 
     def announce(to, carry):
         pl.semaphore_signal(barrier, inc=1, device_id={"bl": z_peer(to)}, device_id_type=MESH)
         return carry
 
-    lax.fori_loop(z + 1, NZ, announce, 0)
-    for k in range(1, NY):
-        peer, to = y_peer(k)
-
-        @pl.when(rank_of(to) > rank)
-        def _():
-            pl.semaphore_signal(barrier, inc=1, device_id={"bl": peer}, device_id_type=MESH)
-
-    @pl.when(core == 0)
+    lax.fori_loop(jnp.where(z == 0, NZ, z + 1), NZ, announce, 0)
+
+    @pl.when((z > 0) & (upper == 0))
+    def _():
+        announce(0, 0)
+
+    pl.when((upper == 0) & (second == 0))(lambda: tell_beside(barrier))
+
+    @pl.when((upper == 1) & (core == 0))
     def _():
         pl.semaphore_signal(barrier, inc=1, device_id={"bl": other}, device_id_type=MESH)
 
@@ -117,7 +119,7 @@
         for peer in chan_peers:
             pl.semaphore_signal(barrier, inc=1, device_id={"chan": peer}, device_id_type=MESH)
 
-    earlier = z + rank + core + 2 * odd
+    earlier = jnp.where(z == 0, HALF - 1, z - 1) + (1 - upper) * 3 * second + upper * core + 2 * odd
 
     @pl.when(earlier > 0)
     def _():
@@ -127,15 +129,10 @@
         pl.semaphore_signal(ready_z.at[z], inc=1, device_id={"bl": z_peer(to)}, device_id_type=MESH)
         return carry
 
-    lax.fori_loop(upper * (HALF - 1), z, tell_z, 0)
-    for k in range(1, NY):
-        peer, to = y_peer(k)
-
-        @pl.when(rank_of(to) < rank)
-        def _():
-            pl.semaphore_signal(ready_y, inc=1, device_id={"bl": peer}, device_id_type=MESH)
-
-    @pl.when(core == 1)
+    lax.fori_loop(1 + upper * (HALF - 2), z, tell_z, 0)
+    pl.when((upper == 0) & (second == 1))(lambda: tell_beside(ready_y))
+
+    @pl.when((upper == 1) & (core == 1))
     def _():
         pl.semaphore_signal(ready_c, inc=1, device_id={"bl": other}, device_id_type=MESH)
 
@@ -149,9 +146,15 @@
         to_bl(mine, mine, zs.at[0], zr.at[z], z_peer(to)).start()
         return carry
 
-    lax.fori_loop(0, z, send_down, 0)
+    lax.fori_loop(1, jnp.where(z == 0, HALF, z), send_down, 0)
     for load in loads[1:]:
         load.start()
+
+    @pl.when((upper == 0) & (second == 0))
+    def _():
+        pl.semaphore_wait(ready_y, 3)
+        tell_beside(ready_y)
+
 
     loads[3].wait()
     lane = lax.broadcasted_iota(jnp.int32, (8, LANES), 1)
@@ -253,23 +256,44 @@
             dst[...] = picked if first else dst[...] + picked
 
     def line(at):
-        for to in range(at + 1, at // HALF * HALF + HALF):
+        for to in range(at + 1, at // HALF * HALF + HALF) if at else ():
             send_up(to, at, 1)
-
-        @pl.when(rank < NY - 1)
-        def _():
-            pl.semaphore_wait(ready_y, NY - 1 - rank)
-
+        if at < HALF:
+
+            @pl.when(second == 1)
+            def _():
+                pl.semaphore_wait(ready_y, 3)
+
+        else:
+            pl.semaphore_wait(ready_y, 1)
+        if at == HALF - 1:
+            pl.semaphore_wait(ready_z.at[HALF], 1)
+        if at in (HALF - 1, HALF):
+            for k in (2, 1, 3):
+                pl.semaphore_signal(hub, inc=1, device_id={"bl": y_peer(k)[0]}, device_id_type=MESH)
+        if at == HALF:
+            pl.semaphore_wait(hub, NY - 1)
+            for to in (7, 6, 5):
+                pl.semaphore_signal(ready_y, inc=1, device_id={"bl": z_peer(to)}, device_id_type=MESH)
         pass_on(at)
         if at < HALF:
-            for v in range(HALF):
+            for v in (1, 2, 3, 0):
                 if v != at:
                     take_in(v)
+            if at:
+                send_down(0, 0)
             if at == HALF - 1:
-                for to in (4, 7, 6, 5):
+                pl.semaphore_wait(hub, NY - 1)
+                pl.semaphore_signal(ready_y, inc=1, device_id={"bl": z_peer(HALF)}, device_id_type=MESH)
+                lower = pieces(0, HALF)
+                to_bl(lower, lower, zs.at[1], zr.at[0], z_peer(HALF)).start()
+                for to in (7, 6, 5):
                     send_up(to, 0, HALF)
             for v in range(HALF, NZ):
                 take_in(v)
+                if at == 1:
+                    piece = pieces(v, 1)
+                    to_bl(piece, piece, zs.at[1], zr.at[v], z_peer(0)).start()
         else:
             for v in range(HALF, NZ):
                 if v != at:
@@ -279,7 +303,7 @@
     for at in range(NZ):
         pl.when(z == at)(functools.partial(line, at))
 
-    @pl.when(core == 0)
+    @pl.when((upper == 1) & (core == 0))
     def _():
         pl.semaphore_wait(ready_c, 1)
 
@@ -440,7 +464,7 @@
         edge.wait_send()
 
     def left(at):
-        for sem, count in ((0, at), (1, (3, 2, 1, 16, 3, 2, 1, 0)[at])):
+        for sem, count in ((0, (3, 1, 2, 3, 3, 4, 5, 6)[at]), (1, (0, 6, 1, 16, 3, 2, 1, 0)[at])):
             if count:
                 sent = part.at[pl.ds(0, count), 0, 0] if count <= NZ else part.at[pl.ds(0, count // NY), 0]
                 to_bl(sent, sent, zs.at[sem], rzr.at[0], other).wait_send()
@@ -481,7 +505,7 @@
             vmem((8, 128), F32), vmem((2, 8, 128), F32),
             dma((8,)), dma((2,)), dma((NZ,)), dma((1,)), dma((2,)), dma((1,)), dma((2,)), dma((2,)), dma((2,)),
             dma((1,)), dma((DIRECT,)), dma((1,)), dma((NZ,)), dma((1,)), dma((NZ,)), dma((1,)), dma((1,)),
-            flag((NZ,)), flag, flag,
+            flag((NZ,)), flag, flag, flag,
         ],
         compiler_params=pltpu.CompilerParams(
             collective_id=0, has_side_effects=True, vmem_limit_bytes=58 * 1024 * 1024

time: 37.6 us -> 36.9 us (0.981)
  Pallas kernels: 35.4 us -> 34.7 us
    pallas_call x1, Pallas kernels: 35.4 us -> 34.7 us  [local(): pl.pallas_call(kernel, out_shape=(vmem((8, TIMES, CHANNELS, 8), F32), vme...]
where the time goes in v4:
time: 36.9 us; the launch traced here: 36.8 us
  Pallas kernels  34.7 us (94%)
  local copies, waits for them, and re-layouts  1.45 us (4%)
  between operations  0.64 us (2%)
    pallas_call x1, Pallas kernels, local(): pl.pallas_call(kernel, out_shape=(vmem((8, TIMES, CHANNELS, 8), F32), vme...  34.7 us
    unnamed x2, local copies, waits for them, and re-layouts  1.45 us

profile of v4, /device:TPU:1, one launch (start us, length us, event | category | flops | bytes accessed | tf_op | source)
XLA Modules:
  0.0 36.8 jit_solution(11069523010531144938)
XLA Ops:
  0.6 34.7 %shard_map.95 = (f32[8,4,8,8]{3,2,1,0:T(8,128)S(1)}, f32[8,4,8,512]{3,2,1,0:T(8,128)S(1)}) custom-call(f32[8,4,8,512]{3,2,1,0:T(8,128)} %meas_h.1, f32[8,4,8,512]{3,2,1,0:T(8,128)} %model_h.1, f32[4,8,512]{2,1,0:T(8,128)} %imp_h.1, s32[1,512]{1,0:T(1,128)} %tally_h.1, s32[1,512]{1,0:T(1,128)} %bitcast.2, s32[1,512]{1,0:T(1,128)} %bitcast.3, ...), custom_call_target="tpu_custom_call" | custom-call | tf_op jit(solution)/shard_map/pallas_call | solution.py:493
  35.3 0.7 %copy.12 = f32[8,4,8,8]{3,2,1,0:T(8,128)} copy(f32[8,4,8,8]{3,2,1,0:T(8,128)S(1)} %get-tuple-element.2) | data formatting | bytes 16384
  36.0 0.8 %copy.13 = f32[8,4,8,512]{3,2,1,0:T(8,128)} copy(f32[8,4,8,512]{3,2,1,0:T(8,128)S(1)} %get-tuple-element.3) | data formatting | bytes 1048576

commit v5 on v4

--- a/solution.py
+++ b/solution.py
@@ -102,12 +102,8 @@
         pl.semaphore_signal(barrier, inc=1, device_id={"bl": z_peer(to)}, device_id_type=MESH)
         return carry
 
-    lax.fori_loop(jnp.where(z == 0, NZ, z + 1), NZ, announce, 0)
-
-    @pl.when((z > 0) & (upper == 0))
-    def _():
-        announce(0, 0)
-
+    lax.fori_loop(0, (1 - upper) * z, announce, 0)
+    lax.fori_loop(jnp.where(z == 0, NZ, jnp.maximum(z + 1, HALF)), NZ, announce, 0)
     pl.when((upper == 0) & (second == 0))(lambda: tell_beside(barrier))
 
     @pl.when((upper == 1) & (core == 0))
@@ -119,7 +115,7 @@
         for peer in chan_peers:
             pl.semaphore_signal(barrier, inc=1, device_id={"chan": peer}, device_id_type=MESH)
 
-    earlier = jnp.where(z == 0, HALF - 1, z - 1) + (1 - upper) * 3 * second + upper * core + 2 * odd
+    earlier = upper * (z - 1) + (1 - upper) * (HALF - 1 - z) + (1 - upper) * 3 * second + upper * core + 2 * odd
 
     @pl.when(earlier > 0)
     def _():
@@ -129,7 +125,7 @@
         pl.semaphore_signal(ready_z.at[z], inc=1, device_id={"bl": z_peer(to)}, device_id_type=MESH)
         return carry
 
-    lax.fori_loop(1 + upper * (HALF - 2), z, tell_z, 0)
+    lax.fori_loop(HALF - 1, z, tell_z, 0)
     pl.when((upper == 0) & (second == 1))(lambda: tell_beside(ready_y))
 
     @pl.when((upper == 1) & (core == 1))
@@ -142,11 +138,11 @@
 
     mine = table.at[z, core, y]
 
-    def send_down(to, carry):
+    def send_own(to, carry):
         to_bl(mine, mine, zs.at[0], zr.at[z], z_peer(to)).start()
         return carry
 
-    lax.fori_loop(1, jnp.where(z == 0, HALF, z), send_down, 0)
+    lax.fori_loop(1 + (1 - upper) * z, upper * z + (1 - upper) * HALF, send_own, 0)
     for load in loads[1:]:
         load.start()
 
@@ -199,10 +195,10 @@
     row1, row2 = to_row(one[...]), to_row(two[...])
 
     def hot_body(i, carry):
-        base = pl.multiple_of(i * 32, 32)
-        index = lax.broadcasted_iota(jnp.int32, (32, PAIRS), 0) + base
-        hot1[pl.ds(base, 32), :] = jnp.where(index == row1, 1.0, 0.0).astype(BF16)
-        hot2[pl.ds(base, 32), :] = jnp.where(index == row2, 1.0, 0.0).astype(BF16)
+        index = lax.broadcasted_iota(jnp.int32, (32, PAIRS), 0) + i * 32
+        v, half = lax.div(i, NC), lax.rem(i, NC)
+        hot1[v, half] = jnp.where(index == row1, 1.0, 0.0).astype(BF16)
+        hot2[v, half] = jnp.where(index == row2, 1.0, 0.0).astype(BF16)
         return carry
 
     lax.fori_loop(0, 16, hot_body, 0)
@@ -243,20 +239,18 @@
         to_bl(four, four, cs.at[0], cr.at[half], other).start()
 
     def pick(half, first):
-        four = table.at[pl.ds(half * HALF, HALF), 1 - core]
-        to_bl(four, four, cs.at[0], cr.at[half], other).wait_recv()
-        flipped = jnp.transpose(table[pl.ds(half * HALF, HALF)].reshape(256, LANES))
+        flipped = jnp.transpose(table[:, half].reshape(256, LANES))
         g_high, g_low = halves(flipped)
-        rows = pl.ds(pl.multiple_of(half * 256, 256), 256)
         for hot, dst in ((hot1, gp), (hot2, gq)):
-            picked = jnp.dot(g_high, hot[rows, :], preferred_element_type=F32) + jnp.dot(
-                g_low, hot[rows, :], preferred_element_type=F32
+            rows = hot[:, half].reshape(256, PAIRS)
+            picked = jnp.dot(g_high, rows, preferred_element_type=F32) + jnp.dot(
+                g_low, rows, preferred_element_type=F32
             )
             picked = picked.reshape(8, TIMES, CHANNELS, PAIRS)
             dst[...] = picked if first else dst[...] + picked
 
     def line(at):
-        for to in range(at + 1, at // HALF * HALF + HALF) if at else ():
+        for to in range(at + 1, NZ) if at >= HALF else ():
             send_up(to, at, 1)
         if at < HALF:
 
@@ -277,17 +271,17 @@
                 pl.semaphore_signal(ready_y, inc=1, device_id={"bl": z_peer(to)}, device_id_type=MESH)
         pass_on(at)
         if at < HALF:
-            for v in (1, 2, 3, 0):
+            for v in (3, 2, 1, 0):
                 if v != at:
                     take_in(v)
-            if at:
-                send_down(0, 0)
+                if v < at:
+                    send_own(v, 0)
             if at == HALF - 1:
                 pl.semaphore_wait(hub, NY - 1)
                 pl.semaphore_signal(ready_y, inc=1, device_id={"bl": z_peer(HALF)}, device_id_type=MESH)
                 lower = pieces(0, HALF)
                 to_bl(lower, lower, zs.at[1], zr.at[0], z_peer(HALF)).start()
-                for to in (7, 6, 5):
+                for to in (5, 6, 7):
                     send_up(to, 0, HALF)
             for v in range(HALF, NZ):
                 take_in(v)
@@ -309,8 +303,11 @@
 
     share(upper)
     share(1 - upper)
-    pick(upper, True)
-    pick(1 - upper, False)
+    pick(core, True)
+    for half in range(2):
+        four = table.at[pl.ds(half * HALF, HALF), 1 - core]
+        to_bl(four, four, cs.at[0], cr.at[half], other).wait_recv()
+    pick(1 - core, False)
 
     def compute(i, carry):
         t = lax.div(i, 4)
@@ -352,26 +349,30 @@
             gq[k + 4, t, :, at] = second[k][1]
         return carry
 
-    lax.fori_loop(0, 16, compute, 0)
+    lax.fori_loop(0, 16, compute, 0, unroll=2)
 
     p_high, p_low = halves(gp[...].reshape(LANES, PAIRS))
     q_high, q_low = halves(gq[...].reshape(LANES, PAIRS))
     nt = (((1,), (1,)), ((), ()))
 
     def add_up(v, count):
-        rows = pl.ds(v * 64, count * 64)
-        h1, h2 = hot1[rows, :], hot2[rows, :]
+        h1, h2 = (hot[pl.ds(v, count)].reshape(count * 64, PAIRS) for hot in (hot1, hot2))
         total = lax.dot_general(h1, p_high, nt, preferred_element_type=F32)
         total += lax.dot_general(h1, p_low, nt, preferred_element_type=F32)
         total += lax.dot_general(h2, q_high, nt, preferred_element_type=F32)
         total += lax.dot_general(h2, q_low, nt, preferred_element_type=F32)
         part[pl.ds(v, count)] = total.reshape(count, NC, NY, 8, LANES)
 
-    def hand_over(v, carry):
+    def from_end(v):
+        return v + odd * (NZ - 1 - 2 * v)
+
+    def hand_over(step, carry):
+        v = from_end(step)
         to_bl(part.at[v, 1 - core], got_c.at[v], rcs.at[0], rcr.at[v], other).start()
         return carry
 
-    def along_y(v, carry):
+    def along_y(step, carry):
+        v = from_end(step)
         got = got_c.at[v]
         to_bl(got, got, rcs.at[0], rcr.at[v], other).wait_recv()
         part[v, core] = part[v, core] + got_c[v]
@@ -385,32 +386,35 @@
         def _():
             to_bl(part.at[v, core, y], got_z.at[z], rzs.at[0], rzr.at[0], z_peer(v)).start()
 
-    def along_z(v, carry):
+    def along_z(step, carry):
+        v = from_end(step)
         got = got_y.at[v]
         to_bl(got, got, rys.at[0], ryr.at[v], other).wait_recv()
         part[v, core, y] = part[v, core, y] + got_y[v, 0] + (got_y[v, 1] + got_y[v, 2])
         send_on(v)
         return carry
 
-    add_up(0, DIRECT)
+    add_up(odd * (NZ - DIRECT), DIRECT)
     for v in range(DIRECT):
+        at_v = from_end(v)
         for slot, (dy, dc) in enumerate(((2, 0), (2, 1), (1, 0), (1, 1), (3, 0), (3, 1), (0, 1))):
             to_y, to_core = lax.rem(y + dy, NY), lax.rem(core + dc, NC)
             to_bl(
-                part.at[v, to_core, to_y], got_0.at[v, slot], r0s.at[0], r0r.at[v],
+                part.at[at_v, to_core, to_y], got_0.at[v, slot], r0s.at[0], r0r.at[v],
                 join_index(to_y, z, to_core),
             ).start()
-    add_up(DIRECT, NZ - DIRECT)
+    add_up((1 - odd) * DIRECT, NZ - DIRECT)
     lax.fori_loop(DIRECT, NZ, hand_over, 0)
     lax.fori_loop(DIRECT, NZ, along_y, 0)
     for v in range(DIRECT):
         got = got_0.at[v]
         to_bl(got, got, r0s.at[0], r0r.at[v], other).wait_recv()
-        total = part[v, core, y]
+        at_v = from_end(v)
+        total = part[at_v, core, y]
         for slot in range(7):
             total = total + got_0[v, slot]
-        part[v, core, y] = total
-        send_on(v)
+        part[at_v, core, y] = total
+        send_on(at_v)
     lax.fori_loop(DIRECT, NZ, along_z, 0)
     got_z[z] = part[z, core, y]
 
@@ -464,7 +468,7 @@
         edge.wait_send()
 
     def left(at):
-        for sem, count in ((0, (3, 1, 2, 3, 3, 4, 5, 6)[at]), (1, (0, 6, 1, 16, 3, 2, 1, 0)[at])):
+        for sem, count in ((0, (3, 3, 3, 3, 3, 4, 5, 6)[at]), (1, (0, 4, 0, 16, 3, 2, 1, 0)[at])):
             if count:
                 sent = part.at[pl.ds(0, count), 0, 0] if count <= NZ else part.at[pl.ds(0, count // NY), 0]
                 to_bl(sent, sent, zs.at[sem], rzr.at[0], other).wait_send()
@@ -483,6 +487,17 @@
     to_bl(most, most, rys.at[0], rzr.at[0], other).wait_send()
 
 
+def hand_out(updated, residual, updated_h, residual_h, sem):
+    copies = [
+        pltpu.make_async_copy(residual, residual_h, sem.at[0]),
+        pltpu.make_async_copy(updated, updated_h, sem.at[1]),
+    ]
+    for copy in copies:
+        copy.start()
+    for copy in copies:
+        copy.wait()
+
+
 def local(meas, model, imp, tally, one, two, gains, tvw):
     big = (8, TIMES, CHANNELS, PAIRS)
     vmem = pltpu.VMEM
@@ -490,7 +505,7 @@
     flag = pltpu.SemaphoreType.REGULAR
     any_spec = pl.BlockSpec(memory_space=pl.ANY)
     vmem_spec = pl.BlockSpec(memory_space=pltpu.VMEM)
-    return pl.pallas_call(
+    updated, residual = pl.pallas_call(
         kernel,
         out_shape=(vmem((8, TIMES, CHANNELS, 8), F32), vmem(big, F32)),
         in_specs=[any_spec] * 8,
@@ -499,7 +514,7 @@
             vmem(big, F32), vmem(big, F32), vmem((TIMES, CHANNELS, PAIRS), F32),
             vmem((1, PAIRS), jnp.int32), vmem((1, PAIRS), jnp.int32), vmem((1, PAIRS), jnp.int32),
             vmem((8, TIMES, CHANNELS, 8), F32), vmem((CHANNELS, 8), F32),
-            vmem((NZ, NC, NY, 8, LANES), F32), vmem((STATIONS, PAIRS), BF16), vmem((STATIONS, PAIRS), BF16),
+            vmem((NZ, NC, NY, 8, LANES), F32), vmem((NZ, NC, 32, PAIRS), BF16), vmem((NZ, NC, 32, PAIRS), BF16),
             vmem(big, F32), vmem(big, F32), vmem((NZ, NC, NY, 8, LANES), F32),
             vmem((DIRECT, 7, 8, LANES), F32), vmem((NZ, NY, 8, LANES), F32), vmem((NZ, NY - 1, 8, LANES), F32), vmem((NZ, 8, LANES), F32),
             vmem((8, 128), F32), vmem((2, 8, 128), F32),
@@ -511,6 +526,14 @@
             collective_id=0, has_side_effects=True, vmem_limit_bytes=58 * 1024 * 1024
         ),
     )(meas, model, imp, tally, one.reshape(1, PAIRS), two.reshape(1, PAIRS), gains, tvw)
+    held = [pltpu.with_memory_space_constraint(x, pltpu.VMEM) for x in (updated, residual)]
+    return pl.pallas_call(
+        hand_out,
+        out_shape=(jax.ShapeDtypeStruct(updated.shape, F32), jax.ShapeDtypeStruct(residual.shape, F32)),
+        in_specs=[vmem_spec, vmem_spec],
+        out_specs=(any_spec, any_spec),
+        scratch_shapes=[dma((2,))],
+    )(*held)
 
 
 def solution(mesh):

time: 36.9 us -> 36 us (0.976)
  local copies, waits for them, and re-layouts: 1.45 us -> 0 us
  Pallas kernels: 34.7 us -> 35.2 us
    unnamed x2 -> x0, local copies, waits for them, and re-layouts: 1.45 us -> none
    pallas_call x0 -> x1, Pallas kernels: none -> 0.85 us  [local(): pl.pallas_call(hand_out, out_shape=(jax.ShapeDtypeStruct(updated.shape, F...]
where the time goes in v5:
time: 36 us; the launch traced here: 35.9 us
  Pallas kernels  35.2 us (98%)
  between operations  0.64 us (2%)
    pallas_call x1, Pallas kernels, local(): pl.pallas_call(kernel, out_shape=(vmem((8, TIMES, CHANNELS, 8), F32), vme...  34.4 us
    pallas_call x1, Pallas kernels, local(): pl.pallas_call(hand_out, out_shape=(jax.ShapeDtypeStruct(updated.shape, F...  0.85 us

profile of v5, /device:TPU:1, one launch (start us, length us, event | category | flops | bytes accessed | tf_op | source)
XLA Modules:
  0.0 35.9 jit_solution(18315068138770712096)
XLA Ops:
  0.6 34.4 %shard_map.95 = (f32[8,4,8,8]{3,2,1,0:T(8,128)S(1)}, f32[8,4,8,512]{3,2,1,0:T(8,128)S(1)}) custom-call(f32[8,4,8,512]{3,2,1,0:T(8,128)} %meas_h.1, f32[8,4,8,512]{3,2,1,0:T(8,128)} %model_h.1, f32[4,8,512]{2,1,0:T(8,128)} %imp_h.1, s32[1,512]{1,0:T(1,128)} %tally_h.1, s32[1,512]{1,0:T(1,128)} %bitcast.2, s32[1,512]{1,0:T(1,128)} %bitcast.3, ...), custom_call_target="tpu_custom_call" | custom-call | tf_op jit(solution)/shard_map/pallas_call | solution.py:508
  35.0 0.8 %shard_map.96 = (f32[8,4,8,8]{3,2,1,0:T(8,128)}, f32[8,4,8,512]{3,2,1,0:T(8,128)}) custom-call(f32[8,4,8,8]{3,2,1,0:T(8,128)S(1)} %get-tuple-element.4.updated, f32[8,4,8,512]{3,2,1,0:T(8,128)S(1)} %get-tuple-element.5.residual), custom_call_target="tpu_custom_call" | custom-call | tf_op jit(solution)/shard_map/pallas_call | solution.py:530

commit v6 on v5

--- a/solution.py
+++ b/solution.py
@@ -355,16 +355,22 @@
     q_high, q_low = halves(gq[...].reshape(LANES, PAIRS))
     nt = (((1,), (1,)), ((), ()))
 
-    def add_up(v, count):
-        h1, h2 = (hot[pl.ds(v, count)].reshape(count * 64, PAIRS) for hot in (hot1, hot2))
+    def add_up(places):
+        h1, h2 = (
+            jnp.concatenate([hot[v].reshape(64, PAIRS) for v in places]) for hot in (hot1, hot2)
+        )
         total = lax.dot_general(h1, p_high, nt, preferred_element_type=F32)
         total += lax.dot_general(h1, p_low, nt, preferred_element_type=F32)
         total += lax.dot_general(h2, q_high, nt, preferred_element_type=F32)
         total += lax.dot_general(h2, q_low, nt, preferred_element_type=F32)
-        part[pl.ds(v, count)] = total.reshape(count, NC, NY, 8, LANES)
+        for i, v in enumerate(places):
+            part[v] = total[i * 64 : i * 64 + 64].reshape(NC, NY, 8, LANES)
 
     def from_end(v):
-        return v + odd * (NZ - 1 - 2 * v)
+        if isinstance(v, int):
+            return v + odd * ((v // 2 if v % 2 else NZ - 1 - v // 2) - v)
+        far = lax.rem(v, 2)
+        return v + odd * (lax.div(v, 2) * (2 * far - 1) + (1 - far) * (NZ - 1) - v)
 
     def hand_over(step, carry):
         v = from_end(step)
@@ -394,7 +400,7 @@
         send_on(v)
         return carry
 
-    add_up(odd * (NZ - DIRECT), DIRECT)
+    add_up([from_end(v) for v in range(DIRECT)])
     for v in range(DIRECT):
         at_v = from_end(v)
         for slot, (dy, dc) in enumerate(((2, 0), (2, 1), (1, 0), (1, 1), (3, 0), (3, 1), (0, 1))):
@@ -403,7 +409,7 @@
                 part.at[at_v, to_core, to_y], got_0.at[v, slot], r0s.at[0], r0r.at[v],
                 join_index(to_y, z, to_core),
             ).start()
-    add_up((1 - odd) * DIRECT, NZ - DIRECT)
+    add_up([DIRECT - odd + v for v in range(NZ - DIRECT)])
     lax.fori_loop(DIRECT, NZ, hand_over, 0)
     lax.fori_loop(DIRECT, NZ, along_y, 0)
     for v in range(DIRECT):

time: 36 us -> 36 us (level)
  no operation moved by 1% of the time
where the time goes in v6:
time: 36 us; the launch traced here: 35.9 us
  Pallas kernels  35.2 us (98%)
  between operations  0.64 us (2%)
    pallas_call x1, Pallas kernels, local(): pl.pallas_call(kernel, out_shape=(vmem((8, TIMES, CHANNELS, 8), F32), vme...  34.4 us
    pallas_call x1, Pallas kernels, local(): pl.pallas_call(hand_out, out_shape=(jax.ShapeDtypeStruct(updated.shape, F...  0.85 us

profile of v6, /device:TPU:1, one launch (start us, length us, event | category | flops | bytes accessed | tf_op | source)
XLA Modules:
  0.0 35.9 jit_solution(14079366362425157908)
XLA Ops:
  0.6 34.4 %shard_map.95 = (f32[8,4,8,8]{3,2,1,0:T(8,128)S(1)}, f32[8,4,8,512]{3,2,1,0:T(8,128)S(1)}) custom-call(f32[8,4,8,512]{3,2,1,0:T(8,128)} %meas_h.1, f32[8,4,8,512]{3,2,1,0:T(8,128)} %model_h.1, f32[4,8,512]{2,1,0:T(8,128)} %imp_h.1, s32[1,512]{1,0:T(1,128)} %tally_h.1, s32[1,512]{1,0:T(1,128)} %bitcast.2, s32[1,512]{1,0:T(1,128)} %bitcast.3, ...), custom_call_target="tpu_custom_call" | custom-call | tf_op jit(solution)/shard_map/pallas_call | solution.py:514
  35.0 0.8 %shard_map.96 = (f32[8,4,8,8]{3,2,1,0:T(8,128)}, f32[8,4,8,512]{3,2,1,0:T(8,128)}) custom-call(f32[8,4,8,8]{3,2,1,0:T(8,128)S(1)} %get-tuple-element.4.updated, f32[8,4,8,512]{3,2,1,0:T(8,128)S(1)} %get-tuple-element.5.residual), custom_call_target="tpu_custom_call" | custom-call | tf_op jit(solution)/shard_map/pallas_call | solution.py:536

commit v7 on v6

--- a/solution.py
+++ b/solution.py
@@ -249,6 +249,10 @@
             picked = picked.reshape(8, TIMES, CHANNELS, PAIRS)
             dst[...] = picked if first else dst[...] + picked
 
+    def tell_plane():
+        pl.semaphore_wait(hub, NY - 1)
+        pl.semaphore_signal(ready_y, inc=1, device_id={"bl": z_peer(HALF)}, device_id_type=MESH)
+
     def line(at):
         for to in range(at + 1, NZ) if at >= HALF else ():
             send_up(to, at, 1)
@@ -272,13 +276,14 @@
         pass_on(at)
         if at < HALF:
             for v in (3, 2, 1, 0):
+                if at == HALF - 1 and v == 0:
+                    pl.when(early)(tell_plane)
                 if v != at:
                     take_in(v)
                 if v < at:
                     send_own(v, 0)
             if at == HALF - 1:
-                pl.semaphore_wait(hub, NY - 1)
-                pl.semaphore_signal(ready_y, inc=1, device_id={"bl": z_peer(HALF)}, device_id_type=MESH)
+                pl.when(jnp.logical_not(early))(tell_plane)
                 lower = pieces(0, HALF)
                 to_bl(lower, lower, zs.at[1], zr.at[0], z_peer(HALF)).start()
                 for to in (5, 6, 7):

time: 36 us -> 35.6 us (0.989)
    pallas_call x1, Pallas kernels: 34.4 us -> 34 us  [local(): pl.pallas_call(kernel, out_shape=(vmem((8, TIMES, CHANNELS, 8), F32), vme...]
where the time goes in v7:
time: 35.6 us; the launch traced here: 35.5 us
  Pallas kernels  34.9 us (98%)
  between operations  0.64 us (2%)
    pallas_call x1, Pallas kernels, local(): pl.pallas_call(kernel, out_shape=(vmem((8, TIMES, CHANNELS, 8), F32), vme...  34 us
    pallas_call x1, Pallas kernels, local(): pl.pallas_call(hand_out, out_shape=(jax.ShapeDtypeStruct(updated.shape, F...  0.85 us

profile of v7, /device:TPU:1, one launch (start us, length us, event | category | flops | bytes accessed | tf_op | source)
XLA Modules:
  0.0 35.5 jit_solution(9417869887471949560)
XLA Ops:
  0.6 34.0 %shard_map.95 = (f32[8,4,8,8]{3,2,1,0:T(8,128)S(1)}, f32[8,4,8,512]{3,2,1,0:T(8,128)S(1)}) custom-call(f32[8,4,8,512]{3,2,1,0:T(8,128)} %meas_h.1, f32[8,4,8,512]{3,2,1,0:T(8,128)} %model_h.1, f32[4,8,512]{2,1,0:T(8,128)} %imp_h.1, s32[1,512]{1,0:T(1,128)} %tally_h.1, s32[1,512]{1,0:T(1,128)} %bitcast.2, s32[1,512]{1,0:T(1,128)} %bitcast.3, ...), custom_call_target="tpu_custom_call" | custom-call | tf_op jit(solution)/shard_map/pallas_call | solution.py:519
  34.7 0.8 %shard_map.96 = (f32[8,4,8,8]{3,2,1,0:T(8,128)}, f32[8,4,8,512]{3,2,1,0:T(8,128)}) custom-call(f32[8,4,8,8]{3,2,1,0:T(8,128)S(1)} %get-tuple-element.4.updated, f32[8,4,8,512]{3,2,1,0:T(8,128)S(1)} %get-tuple-element.5.residual), custom_call_target="tpu_custom_call" | custom-call | tf_op jit(solution)/shard_map/pallas_call | solution.py:541

commit v8 on v7

--- a/solution.py
+++ b/solution.py
@@ -208,9 +208,6 @@
     keep = lax.broadcasted_iota(jnp.int32, (CHANNELS, PAIRS), 0) < CHANNELS - tally[...]
     for t in range(TIMES):
         imp[t] = jnp.where(keep, imp[t], 0.0)
-    loads[6].wait()
-    loads[7].wait()
-
     def pieces(v, count):
         return table.at[v, core, y] if count == 1 else table.at[pl.ds(v, count), core, y]
 
@@ -354,6 +351,8 @@
             gq[k + 4, t, :, at] = second[k][1]
         return carry
 
+    loads[6].wait()
+    loads[7].wait()
     lax.fori_loop(0, 16, compute, 0, unroll=2)
 
     p_high, p_low = halves(gp[...].reshape(LANES, PAIRS))
@@ -500,8 +499,8 @@
 
 def hand_out(updated, residual, updated_h, residual_h, sem):
     copies = [
-        pltpu.make_async_copy(residual, residual_h, sem.at[0]),
-        pltpu.make_async_copy(updated, updated_h, sem.at[1]),
+        pltpu.make_async_copy(updated, updated_h, sem.at[0]),
+        pltpu.make_async_copy(residual, residual_h, sem.at[1]),
     ]
     for copy in copies:
         copy.start()

time: 35.6 us -> 35.6 us (level)
  no operation moved by 1% of the time
where the time goes in v8:
time: 35.6 us; the launch traced here: 35.5 us
  Pallas kernels  34.9 us (98%)
  between operations  0.64 us (2%)
    pallas_call x1, Pallas kernels, local(): pl.pallas_call(kernel, out_shape=(vmem((8, TIMES, CHANNELS, 8), F32), vme...  34 us
    pallas_call x1, Pallas kernels, local(): pl.pallas_call(hand_out, out_shape=(jax.ShapeDtypeStruct(updated.shape, F...  0.86 us

profile of v8, /device:TPU:1, one launch (start us, length us, event | category | flops | bytes accessed | tf_op | source)
XLA Modules:
  0.0 35.5 jit_solution(13754283128896664893)
XLA Ops:
  0.6 34.0 %shard_map.95 = (f32[8,4,8,8]{3,2,1,0:T(8,128)S(1)}, f32[8,4,8,512]{3,2,1,0:T(8,128)S(1)}) custom-call(f32[8,4,8,512]{3,2,1,0:T(8,128)} %meas_h.1, f32[8,4,8,512]{3,2,1,0:T(8,128)} %model_h.1, f32[4,8,512]{2,1,0:T(8,128)} %imp_h.1, s32[1,512]{1,0:T(1,128)} %tally_h.1, s32[1,512]{1,0:T(1,128)} %bitcast.2, s32[1,512]{1,0:T(1,128)} %bitcast.3, ...), custom_call_target="tpu_custom_call" | custom-call | tf_op jit(solution)/shard_map/pallas_call | solution.py:518
  34.7 0.9 %shard_map.96 = (f32[8,4,8,8]{3,2,1,0:T(8,128)}, f32[8,4,8,512]{3,2,1,0:T(8,128)}) custom-call(f32[8,4,8,8]{3,2,1,0:T(8,128)S(1)} %get-tuple-element.4.updated, f32[8,4,8,512]{3,2,1,0:T(8,128)S(1)} %get-tuple-element.5.residual), custom_call_target="tpu_custom_call" | custom-call | tf_op jit(solution)/shard_map/pallas_call | solution.py:540

commit v9 on v7

--- a/solution.py
+++ b/solution.py
@@ -416,7 +416,7 @@
             ).start()
     add_up([DIRECT - odd + v for v in range(NZ - DIRECT)])
     lax.fori_loop(DIRECT, NZ, hand_over, 0)
-    lax.fori_loop(DIRECT, NZ, along_y, 0)
+    lax.fori_loop(DIRECT, NZ - 3, along_y, 0)
     for v in range(DIRECT):
         got = got_0.at[v]
         to_bl(got, got, r0s.at[0], r0r.at[v], other).wait_recv()
@@ -426,6 +426,7 @@
             total = total + got_0[v, slot]
         part[at_v, core, y] = total
         send_on(at_v)
+    lax.fori_loop(NZ - 3, NZ, along_y, 0)
     lax.fori_loop(DIRECT, NZ, along_z, 0)
     got_z[z] = part[z, core, y]
 

time: 35.6 us -> 36.5 us (1.025)
  the two profiles are of different devices: /device:TPU:1 before, /device:TPU:386 now
where the time goes in v9:
time: 36.5 us; the launch traced here: 36.4 us
  Pallas kernels  35.7 us (98%)
  between operations  0.64 us (2%)
    pallas_call x1, Pallas kernels, local(): pl.pallas_call(kernel, out_shape=(vmem((8, TIMES, CHANNELS, 8), F32), vme...  34.9 us
    pallas_call x1, Pallas kernels, local(): pl.pallas_call(hand_out, out_shape=(jax.ShapeDtypeStruct(updated.shape, F...  0.85 us

profile of v9, /device:TPU:386, one launch (start us, length us, event | category | flops | bytes accessed | tf_op | source)
XLA Modules:
  0.0 36.4 jit_solution(16863978615575794973)
XLA Ops:
  0.6 34.9 %shard_map.95 = (f32[8,4,8,8]{3,2,1,0:T(8,128)S(1)}, f32[8,4,8,512]{3,2,1,0:T(8,128)S(1)}) custom-call(f32[8,4,8,512]{3,2,1,0:T(8,128)} %meas_h.1, f32[8,4,8,512]{3,2,1,0:T(8,128)} %model_h.1, f32[4,8,512]{2,1,0:T(8,128)} %imp_h.1, s32[1,512]{1,0:T(1,128)} %tally_h.1, s32[1,512]{1,0:T(1,128)} %bitcast.2, s32[1,512]{1,0:T(1,128)} %bitcast.3, ...), custom_call_target="tpu_custom_call" | custom-call | tf_op jit(solution)/shard_map/pallas_call | solution.py:520
  35.5 0.8 %shard_map.96 = (f32[8,4,8,8]{3,2,1,0:T(8,128)}, f32[8,4,8,512]{3,2,1,0:T(8,128)}) custom-call(f32[8,4,8,8]{3,2,1,0:T(8,128)S(1)} %get-tuple-element.4.updated, f32[8,4,8,512]{3,2,1,0:T(8,128)S(1)} %get-tuple-element.5.residual), custom_call_target="tpu_custom_call" | custom-call | tf_op jit(solution)/shard_map/pallas_call | solution.py:542

commit v10 on v7

--- a/solution.py
+++ b/solution.py
@@ -354,7 +354,7 @@
             gq[k + 4, t, :, at] = second[k][1]
         return carry
 
-    lax.fori_loop(0, 16, compute, 0, unroll=2)
+    lax.fori_loop(0, 16, compute, 0, unroll=4)
 
     p_high, p_low = halves(gp[...].reshape(LANES, PAIRS))
     q_high, q_low = halves(gq[...].reshape(LANES, PAIRS))

time: 35.6 us -> 35.6 us (level)
  no operation moved by 1% of the time
where the time goes in v10:
time: 35.6 us; the launch traced here: 35.5 us
  Pallas kernels  34.8 us (98%)
  between operations  0.64 us (2%)
    pallas_call x1, Pallas kernels, local(): pl.pallas_call(kernel, out_shape=(vmem((8, TIMES, CHANNELS, 8), F32), vme...  34 us
    pallas_call x1, Pallas kernels, local(): pl.pallas_call(hand_out, out_shape=(jax.ShapeDtypeStruct(updated.shape, F...  0.85 us

profile of v10, /device:TPU:1, one launch (start us, length us, event | category | flops | bytes accessed | tf_op | source)
XLA Modules:
  0.0 35.5 jit_solution(16501564998390057366)
XLA Ops:
  0.6 34.0 %shard_map.95 = (f32[8,4,8,8]{3,2,1,0:T(8,128)S(1)}, f32[8,4,8,512]{3,2,1,0:T(8,128)S(1)}) custom-call(f32[8,4,8,512]{3,2,1,0:T(8,128)} %meas_h.1, f32[8,4,8,512]{3,2,1,0:T(8,128)} %model_h.1, f32[4,8,512]{2,1,0:T(8,128)} %imp_h.1, s32[1,512]{1,0:T(1,128)} %tally_h.1, s32[1,512]{1,0:T(1,128)} %bitcast.2, s32[1,512]{1,0:T(1,128)} %bitcast.3, ...), custom_call_target="tpu_custom_call" | custom-call | tf_op jit(solution)/shard_map/pallas_call | solution.py:519
  34.6 0.8 %shard_map.96 = (f32[8,4,8,8]{3,2,1,0:T(8,128)}, f32[8,4,8,512]{3,2,1,0:T(8,128)}) custom-call(f32[8,4,8,8]{3,2,1,0:T(8,128)S(1)} %get-tuple-element.4.updated, f32[8,4,8,512]{3,2,1,0:T(8,128)S(1)} %get-tuple-element.5.residual), custom_call_target="tpu_custom_call" | custom-call | tf_op jit(solution)/shard_map/pallas_call | solution.py:541
